TPU v7x, 128 devices: a whole 4x4x4 slice. The times are simulated.
128 devices in a mesh: smp: 8 (over y, z_lo), par: 16 (over x, z_hi, core).
Axes of the slice: x: 4, y: 4, z: 4 (z_hi: 2, z_lo: 2; z = z_hi * 2 + z_lo), core: 2. Of those that a mesh axis runs over, the one named last changes fastest.
Arguments:
- log_derivs: bfloat16 [2048, 65536], P('smp', 'par')
- spins: int32 [2048, 100], P('smp'), may hold values from 0 to 1
- hop_energy: float32 [2048], P('smp'), may hold values from -8 to 8
Outputs:
- update: float32 [65536], P('par')
- coeffs: float32 [2048], P('smp')
All inputs are finite; a program needn't handle non-finite values.
Results may differ from a plain program's by a relative error of at most 0.0091.
The roundings to bfloat16 on the way count: a program that leaves them out, or rounds other values in their place, can miss the bound.
Values may be sent and summed in bfloat16 or wider, within the bound.
A program may use at most 192 MiB of HBM per device.

v0:
```python
import jax
import jax.numpy as jnp
from jax import lax
from jax.sharding import PartitionSpec as P

SIDE = 10


def local_energy(spins):
    sigma = (2 * spins - 1).astype(jnp.float32).reshape(-1, SIDE, SIDE)
    right = jnp.roll(sigma, 1, axis=2)
    below = jnp.roll(sigma, 1, axis=1)
    diag_one = jnp.roll(below, 1, axis=2)
    diag_two = jnp.roll(below, -1, axis=2)
    nearest = jnp.sum(sigma * right + sigma * below, axis=(1, 2))
    second = jnp.sum(sigma * diag_one + sigma * diag_two, axis=(1, 2))
    return 0.25 * nearest + 0.125 * second


def blocked_cholesky(system):
    order_size = system.shape[0]
    block = 512
    lower = jnp.zeros_like(system)
    for index in range(order_size // block):
        first = index * block
        last = first + block
        done = lower[first:last, :first]
        diag_part = system[first:last, first:last] - jnp.dot(
            done, done.T, precision=lax.Precision.HIGHEST
        )
        diag_factor = jnp.linalg.cholesky(diag_part)
        lower = lower.at[first:last, first:last].set(diag_factor)
        if last < order_size:
            below = system[last:, first:last] - jnp.dot(
                lower[last:, :first], done.T, precision=lax.Precision.HIGHEST
            )
            panel = jax.scipy.linalg.solve_triangular(diag_factor, below.T, lower=True).T
            lower = lower.at[last:, first:last].set(panel)
    return lower


def body(log_derivs, spins, hop_energy):
    rows = log_derivs.shape[0]
    total = rows * lax.axis_size("smp")
    scale = 1.0 / jnp.sqrt(jnp.float32(total))
    energy = local_energy(spins) + hop_energy
    all_energy = lax.all_gather(energy, "smp", axis=0, tiled=True)
    eps = (all_energy - jnp.mean(all_energy)) * scale
    col_sum = lax.psum(jnp.sum(log_derivs.astype(jnp.float32), axis=0), "smp")
    centered = ((log_derivs.astype(jnp.float32) - col_sum / total) * scale).astype(jnp.bfloat16)
    partial_value = lax.dot_general(
        centered,
        lax.all_gather(centered, "smp", axis=0, tiled=True),
        (((1,), (1,)), ((), ())),
        preferred_element_type=jnp.float32,
    )
    row_block = lax.psum(partial_value, "par")
    gram = lax.all_gather(row_block, "smp", axis=0, tiled=True)
    system = gram + 0.2 * jnp.eye(total, dtype=jnp.float32)
    factor = blocked_cholesky(system)
    solved = jax.scipy.linalg.cho_solve((factor, True), eps)
    start = lax.axis_index("smp") * rows
    mine = lax.dynamic_slice_in_dim(solved, start, rows, 0)
    local_term = jnp.dot(mine, centered.astype(jnp.float32), precision=lax.Precision.HIGHEST)
    update = lax.psum(local_term, "smp")
    return (update, mine)


def solution(mesh):
    placed = (P("smp", "par"), P("smp", None), P("smp"))
    return jax.shard_map(
        body, mesh=mesh, in_specs=placed, out_specs=(P("par"), P("smp")), check_vma=False
    )
```

profile of v0, /device:TPU:1, one launch (start us, length us, event | category | flops | bytes accessed | tf_op | source)
XLA Modules:
  0.0 1784.5 jit_solution(4488104510887295191)
XLA Ops:
  9.1 28.7 %psum.21 = f32[4096]{0:T(1024)S(1)} all-reduce(f32[4096]{0:T(1024)S(1)} %convert_reduce_fusion), channel_id=1, replica_groups=mesh['smp'=8,'par'=16] {'smp'}, use_global_device_ids=true, to_apply=%region_1.2 | all-reduce | flops 4096 | bytes 32768 | tf_op jit(solution)/shard_map/psum | solution.py:49
  37.9 3.4 fusion.2
  41.4 332.1 %all-gather.4.cloned.1.call-done = bf16[2048,4096]{1,0:T(8,128)(2,1)} async-done(((bf16[256,4096]{1,0:T(8,128)(2,1)}), bf16[2048,4096]{1,0:T(8,128)(2,1)}) %all-gather.4.cloned.1.call-update) | async-done | bytes 16777232 | tf_op jit(solution)/shard_map/all_gather | solution.py:53
  373.5 12.5 fusion.298
  386.0 145.1 %all-reduce.4.cloned.1.call-done = f32[256,2048]{0,1:T(8,128)} async-done(((f32[256,2048]{0,1:T(8,128)}), f32[256,2048]{0,1:T(8,128)}) %all-reduce.4.cloned.1.call-update) | async-done | bytes 2097168 | tf_op jit(solution)/shard_map/psum | solution.py:57
  531.6 14.1 all-gather
  547.4 312.4 %all-gather.6.cloned.1.call-done = f32[2048,2048]{0,1:T(8,128)} async-done(((f32[256,2048]{0,1:T(8,128)}), f32[2048,2048]{0,1:T(8,128)}) %all-gather.6.cloned.1.call-update) | async-done | bytes 16777232 | tf_op jit(solution)/shard_map/all_gather | solution.py:58
  859.8 7.3 select_add_fusion
  867.0 5.7 copy-done
  874.7 11.7 cholesky.462
  886.4 9.8 custom-call.52
  897.1 11.7 cholesky.481
  909.0 10.2 custom-call.53
  920.3 11.7 cholesky.502
  932.1 9.8 custom-call.54
  942.7 11.9 cholesky.519
  954.7 3.8 slice_bitcast_fusion
  964.2 8.3 while.11
  972.5 39.3 %custom-call.39 = f32[4,128,128]{1,2,0:T(8,128)S(1)} custom-call(f32[4,128,128]{2,1,0:T(8,128)S(1)} %get-tuple-element.94), custom_call_target="InvertDiagBlocksLowerTriangular" | custom-call | tf_op jit(solution)/shard_map/jit(_solve_triangular)/triangular_solve | solution.py:37
  1020.5 2.7 convolution_subtract_fusion.1
  1027.7 3.1 convolution_subtract_fusion.3
  1034.6 12.1 cholesky.534
  1047.4 9.8 custom-call.55
  1060.4 11.7 cholesky.553
  1075.0 10.7 custom-call.56
  1092.6 11.9 cholesky.574
  1105.2 9.8 custom-call.57
  1117.5 11.7 cholesky.591
  1129.3 9.1 scatter.24
  1146.1 2.6 fusion.119
  1148.7 6.3 fusion.14
  1155.0 8.1 while.12
  1163.9 40.1 %custom-call.40 = f32[4,128,128]{1,2,0:T(8,128)S(1)} custom-call(f32[4,128,128]{2,1,0:T(8,128)} %copy-done.9), custom_call_target="InvertDiagBlocksLowerTriangular" | custom-call | tf_op jit(solution)/shard_map/jit(_solve_triangular)/triangular_solve | solution.py:37
  1210.6 12.0 copy.153
  1222.6 6.0 fusion.30
  1229.2 11.7 cholesky.606
  1241.0 9.8 custom-call.58
  1251.5 11.9 cholesky.625
  1263.7 9.8 custom-call.59
  1274.7 11.7 cholesky.646
  1286.5 9.8 custom-call.60
  1297.5 11.7 cholesky.663
  1315.9 6.0 fusion.38
  1322.0 8.8 while.13
  1330.8 39.3 %custom-call.41 = f32[4,128,128]{1,2,0:T(8,128)S(1)} custom-call(f32[4,128,128]{2,1,0:T(8,128)S(1)} %get-tuple-element.110), custom_call_target="InvertDiagBlocksLowerTriangular" | custom-call | tf_op jit(solution)/shard_map/jit(_solve_triangular)/triangular_solve | solution.py:37
  1374.5 8.6 fusion.43
  1383.8 11.7 cholesky.678
  1395.5 9.8 custom-call.61
  1406.0 11.7 cholesky.697
  1418.1 10.2 custom-call.62
  1429.4 11.7 cholesky.718
  1441.2 9.8 custom-call.63
  1451.8 11.9 cholesky.735
  1470.2 12.4 fusion
  1482.5 56.5 %while.14 = (s32[]{:T(128)}, f32[2048,2048]{0,1:T(8,128)}, s32[16,2]{0,1:T(2,128)S(1)}, f32[16,128,128]{2,1,0:T(8,128)}, s32[]{:T(128)}) while((s32[]{:T(128)}, f32[2048,2048]{0,1:T(8,128)}, s32[16,2]{0,1:T(2,128)S(1)}, f32[16,128,128]{2,1,0:T(8,128)}, s32[]{:T(128)}) %tuple.251), condition=%wide.while_cond.10, body=%wide.while_body.10.sunk | while | flops 2 | bytes 393829 | solution.py:61
  1483.2 2.2 dynamic-slice.87
  1486.7 2.2 dynamic-slice.87
  1490.2 2.2 dynamic-slice.87
  1493.8 2.2 dynamic-slice.87
  1500.8 2.2 dynamic-slice.87
  1504.4 2.2 dynamic-slice.87
  1507.9 2.2 dynamic-slice.87
  1539.0 157.9 %custom-call.42 = f32[16,128,128]{1,2,0:T(8,128)S(1)} custom-call(f32[16,128,128]{2,1,0:T(8,128)} %get-tuple-element.118), custom_call_target="InvertDiagBlocksLowerTriangular" | custom-call | tf_op jit(solution)/shard_map/jit(_cho_solve)/triangular_solve | solution.py:61
  1751.3 26.4 %psum.23 = f32[4096]{0:T(1024)} all-reduce(f32[4096]{0:T(1024)S(1)} %bitcast.851), channel_id=1, replica_groups=mesh['smp'=8,'par'=16] {'smp'}, use_global_device_ids=true, to_apply=%region_14.16 | all-reduce | flops 4096 | bytes 32768 | tf_op jit(solution)/shard_map/psum | solution.py:65
  (514 shorter events, 197.4 us)
Async XLA Ops:
  7.2 366.3 %all-gather.4.cloned.1.call-start = ((), (), s32[]{:S(2)}) async-start(), calls=%async_computation | async-start | bytes 18874368 | tf_op jit(solution)/shard_map/all_gather | solution.py:53
  41.3 489.9 %copy-start.7 = (s32[256,100]{0,1:T(8,128)S(1)}, s32[256,100]{0,1:T(8,128)}, u32[]{:S(2)}) copy-start(s32[256,100]{0,1:T(8,128)} %param.19) | copy-start | bytes 307204
  41.3 490.2 %copy-start.12 = (f32[256]{0:T(256)S(1)}, f32[256]{0:T(256)}, u32[]{:S(2)}) copy-start(f32[256]{0:T(256)} %param.20) | copy-start | bytes 3076
  41.3 489.8 %all-reduce.4.cloned.1.call-start = ((), (), s32[]{:S(2)}) async-start(), calls=%async_computation.1 | async-start | bytes 4194304 | tf_op jit(solution)/shard_map/psum | solution.py:57
  386.0 473.8 %all-gather.6.cloned.1.call-start = ((), (), s32[]{:S(2)}) async-start(), calls=%async_computation.2 | async-start | bytes 18874368 | tf_op jit(solution)/shard_map/all_gather | solution.py:58
  867.0 5.7 copy-start
  1011.8 4.9 copy-start.8
  1025.0 0.9 copy-start.3
  1026.1 1.7 copy-start.2
  1033.6 1.0 copy-start.5
  1034.6 103.8 %copy-start.4 = (f32[128,1536]{1,0:T(8,128)S(1)}, f32[128,1536]{1,0:T(8,128)}, u32[]{:S(2)}) copy-start(f32[128,1536]{1,0:T(8,128)} %copy-done.3) | copy-start | bytes 2359300
  1046.7 0.6 copy-start.10
  1059.7 0.7 copy-start.6
  1087.5 52.8 %copy-start.13 = (f32[128]{0:T(128)S(1)}, f32[128]{0:T(128)}, u32[]{:S(2)}) copy-start(f32[128]{0:T(128)} %get-tuple-element.217) | copy-start | bytes 1540
  1163.2 0.7 copy-start.9
  1470.1 12.4 copy-start.14
  1482.5 267.8 %copy-start.1 = (bf16[256,4096]{1,0:T(8,128)(2,1)S(1)}, bf16[256,4096]{1,0:T(8,128)(2,1)}, u32[]{:S(2)}) copy-start(bf16[256,4096]{1,0:T(8,128)(2,1)} %fusion.2) | copy-start | bytes 6291460
  1750.4 27.4 %copy-start.11 = (f32[256,1]{0,1:T(1,128)}, f32[256,1]{0,1:T(1,128)S(1)}, u32[]{:S(2)}) copy-start(f32[256,1]{0,1:T(1,128)S(1)} %constant_dynamic-slice_fusion.4) | copy-start | bytes 3076
Sparse Core Ops, SparseCore 0:
  41.4 332.0 all-gather.3
  386.1 144.9 all-reduce.3
  532.8 326.9 all-gather.5
where the time goes:
time: 1800 us; the launch traced here: 1780 us
  waiting for transfers between devices  790 us (44%)
  other arithmetic  637 us (35%)
  matrix products  132 us (7%)
  local copies, waits for them, and re-layouts  130 us (7%)
  blocking collectives  69.2 us (4%)
  between operations  26.3 us (1%)
    all_gather x1, waiting for transfers between devices, body(): lax.all_gather(centered, 'smp', axis=0, tiled=True)  332 us
    another operation x59, other arithmetic, blocked_cholesky(): diag_factor = jnp.linalg.cholesky(diag_part)  319 us
    all_gather x1, waiting for transfers between devices, body(): gram = lax.all_gather(row_block, 'smp', axis=0, tiled=True)  312 us
    another operation x3, other arithmetic, body(): solved = jax.scipy.linalg.cho_solve((factor, True), eps)  171 us
    psum x1, waiting for transfers between devices, body(): row_block = lax.psum(partial_value, 'par')  145 us
    another operation x7, other arithmetic, blocked_cholesky(): jax.scipy.linalg.solve_triangular(diag_factor, below.T, lower=True)  124 us
    another operation x140, local copies, waits for them, and re-layouts  81 us
    another operation x62, matrix products, body(): solved = jax.scipy.linalg.cho_solve((factor, True), eps)  51.5 us
  transfers between devices with their start and end apart: 3, of which 3 were waited for; matrix products, arithmetic and copies ran while one was open for 0% of the time, Pallas kernels for 0%

commit v1 on v0

v1 whole, which is shorter than its diff:
```python
import functools
import jax, jax.numpy as jnp
from jax import lax
from jax.experimental import pallas as pl
from jax.experimental.pallas import tpu as pltpu
from jax.sharding import PartitionSpec as P

B = 256
H = 128


def split(x):
    hi = x.astype(jnp.bfloat16)
    return hi, (x - hi.astype(jnp.float32)).astype(jnp.bfloat16)


def dot3(ah, al, bh, bl, dims):
    d = lambda a, b: lax.dot_general(a, b, (dims, ((), ())), preferred_element_type=jnp.float32)
    return d(ah, bh) + (d(ah, bl) + d(al, bh))


NT = ((1,), (1,))
NN = ((1,), (0,))


def mm(a, b, dims):
    return dot3(*split(a), *split(b), dims)


def recip(x):
    r = pl.reciprocal(x, approx=True)
    return r * (2.0 - x * r)


def factor_inverse(S, T, R):
    lane = lax.broadcasted_iota(jnp.int32, (8, H), 1)
    sub = lax.broadcasted_iota(jnp.int32, (8, H), 0)
    out = []
    groups = list(S)
    for p in range(16):
        rows = groups[p]
        lo = 8 * p
        for j in range(8):
            T[8 * j : 8 * j + 8, :] = jnp.broadcast_to(rows[:, lo + j : lo + j + 1], (8, H))
        indiag = (lane >= lo) & (lane < lo + 8)
        Pi = jnp.where(indiag, (lane - lo == sub).astype(jnp.float32), rows)
        R[...] = Pi
        e = {}
        for j in range(8):
            for i in range(j, 8):
                e[i, j] = jnp.broadcast_to(T[8 * j + i : 8 * j + i + 1, :], (8, H))
        Y = [jnp.broadcast_to(R[i : i + 1, :], (8, H)) for i in range(8)]
        m, r, U = {}, [], None
        for k in range(8):
            rk = recip(e[k, k])
            r.append(rk)
            for i in range(k + 1, 8):
                m[i, k] = e[i, k] * rk
            for i in range(k + 1, 8):
                for q in range(k + 1, i + 1):
                    e[i, q] = e[i, q] - m[i, k] * e[q, k]
            for i in range(k + 1, 8):
                Y[i] = Y[i] - m[i, k] * Y[k]
            Uk = Y[k] * lax.rsqrt(e[k, k])
            U = Uk if k == 0 else jnp.where(sub == k, Uk, U)
        out.append(U)
        V = [None] * 8
        for j in range(7, -1, -1):
            v = r[j] * Y[j]
            for k in range(7, j, -1):
                v = v - m[k, j] * V[k]
            V[j] = v
        for g in range(p + 1, 16):
            old = groups[g]
            base = jnp.where(indiag, 0.0, old)
            terms = [jnp.broadcast_to(old[:, lo + j : lo + j + 1], (8, H)) * V[j] for j in range(8)]
            t = ((terms[0] + terms[1]) + (terms[2] + terms[3])) + ((terms[4] + terms[5]) + (terms[6] + terms[7]))
            groups[g] = base - t
    return out


def inverse_block(D, Wref, T, R):
    U = factor_inverse([D[8 * g : 8 * g + 8, :] for g in range(16)], T, R)
    lane = lax.broadcasted_iota(jnp.int32, (8, H), 1)
    sub = lax.broadcasted_iota(jnp.int32, (8, H), 0)
    for g in range(16):
        Wref[8 * g : 8 * g + 8, :] = jnp.where(lane <= sub + 8 * g, U[g], 0.0)


def kernel(n, a_ref, e_ref, x_ref, lhi, llo, c, ec, whi, wlo, D, W, T, R, z):
    nb = n // B

    def inner(k, _):
        rows_k = pl.ds(pl.multiple_of(k * B, B), B)
        for kk in range(nb):
            @pl.when(k == kk)
            def _():
                cols = slice(kk * B, kk * B + B)
                w = kk * B
                if kk == 0:
                    c[...] = a_ref[:, cols]
                    ec[...] = e_ref[:, cols]
                else:
                    bh, bl = lhi[w : w + B, :w], llo[w : w + B, :w]
                    eh, el = lhi[n : n + 16, :w], llo[n : n + 16, :w]
                    ec[...] = e_ref[:, cols] - dot3(eh, el, bh, bl, NT)

                    @pl.loop(kk, nb)
                    def _(i):
                        ri = pl.ds(pl.multiple_of(i * B, B), B)
                        c[ri, :] = a_ref[ri, cols] - dot3(lhi[ri, :w], llo[ri, :w], bh, bl, NT)

        d0 = pl.multiple_of(k * B, B)
        D[0] = c[pl.ds(d0, H), 0:H]
        inverse_block_ref(D, W, T, R, 0)
        c21 = c[pl.ds(d0 + H, H), 0:H]
        W1 = W[0]
        l21 = mm(c21, W1, NT)
        D[1] = c[pl.ds(d0 + H, H), H:B] - mm(l21, l21, NT)
        inverse_block_ref(D, W, T, R, 1)
        W2 = W[1]
        w21 = -mm(W2, mm(l21, W1, NN), NN)
        zero = jnp.zeros((H, H), jnp.float32)
        full = jnp.concatenate(
            [jnp.concatenate([W1, zero], 1), jnp.concatenate([w21, W2], 1)], 0
        )
        wh, wl = split(full)
        whi[k], wlo[k] = wh, wl
        for kk in range(nb):
            @pl.when(k == kk)
            def _():
                cols = slice(kk * B, kk * B + B)

                @pl.loop(kk + 1, nb)
                def _(i):
                    ri = pl.ds(pl.multiple_of(i * B, B), B)
                    ch, cl = split(c[ri, :])
                    lhi[ri, cols], llo[ri, cols] = split(dot3(ch, cl, wh, wl, NT))

                eh, el = split(ec[...])
                y = dot3(eh, el, wh, wl, NT)
                lhi[n : n + 16, cols], llo[n : n + 16, cols] = split(y)
                z[:, cols] = y
        return 0

    lax.fori_loop(0, nb, inner, 0)
    for kk in range(nb - 1, -1, -1):
        cols = slice(kk * B, kk * B + B)
        zh, zl = split(z[:, cols])
        x = dot3(zh, zl, whi[kk], wlo[kk], NN)
        x_ref[:, cols] = x
        if kk > 0:
            xh, xl = split(x)
            z[:, : kk * B] -= dot3(xh, xl, lhi[cols, : kk * B], llo[cols, : kk * B], NN)


def inverse_block_ref(D, W, T, R, h):
    inverse_block(D[h], W.at[h], T, R)


def solve(a, eps):
    n = a.shape[0]
    e = jnp.zeros((16, n), jnp.float32).at[0].set(eps)
    nb = n // B
    vm = pl.BlockSpec(memory_space=pltpu.VMEM)
    x = pl.pallas_call(
        functools.partial(kernel, n),
        out_shape=jax.ShapeDtypeStruct((16, n), jnp.float32),
        in_specs=[vm, vm],
        out_specs=vm,
        scratch_shapes=[
            pltpu.VMEM((n + 16, n), jnp.bfloat16),
            pltpu.VMEM((n + 16, n), jnp.bfloat16),
            pltpu.VMEM((n, B), jnp.float32),
            pltpu.VMEM((16, B), jnp.float32),
            pltpu.VMEM((nb, B, B), jnp.bfloat16),
            pltpu.VMEM((nb, B, B), jnp.bfloat16),
            pltpu.VMEM((2, H, H), jnp.float32),
            pltpu.VMEM((2, H, H), jnp.float32),
            pltpu.VMEM((64, H), jnp.float32),
            pltpu.VMEM((8, H), jnp.float32),
            pltpu.VMEM((16, n), jnp.float32),
        ],
        compiler_params=pltpu.CompilerParams(vmem_limit_bytes=60 * 2**20),
    )(a, e)
    return x[0]


SIDE = 10


def local_energy(spins):
    sigma = (2 * spins - 1).astype(jnp.float32).reshape(-1, SIDE, SIDE)
    right = jnp.roll(sigma, 1, axis=2)
    below = jnp.roll(sigma, 1, axis=1)
    diag_one = jnp.roll(below, 1, axis=2)
    diag_two = jnp.roll(below, -1, axis=2)
    nearest = jnp.sum(sigma * right + sigma * below, axis=(1, 2))
    second = jnp.sum(sigma * diag_one + sigma * diag_two, axis=(1, 2))
    return 0.25 * nearest + 0.125 * second


def body(log_derivs, spins, hop_energy):
    rows = log_derivs.shape[0]
    total = rows * lax.axis_size("smp")
    scale = 1.0 / jnp.sqrt(jnp.float32(total))
    energy = local_energy(spins) + hop_energy
    all_energy = lax.all_gather(energy, "smp", axis=0, tiled=True)
    eps = (all_energy - jnp.mean(all_energy)) * scale
    mine = lax.all_to_all(log_derivs, "smp", split_axis=1, concat_axis=0, tiled=True)
    wide = mine.astype(jnp.float32)
    centered = ((wide - jnp.sum(wide, axis=0) / total) * scale).astype(jnp.bfloat16)
    part = lax.dot_general(centered, centered, (NT, ((), ())), preferred_element_type=jnp.float32)
    block = lax.psum_scatter(part, ("smp", "par"), scatter_dimension=0, tiled=True)
    gram = lax.all_gather(block, ("smp", "par"), axis=0, tiled=True)
    coeffs = solve(gram + 0.2 * jnp.eye(total, dtype=jnp.float32), eps)
    term = jnp.dot(coeffs[None], centered.astype(jnp.float32), precision=lax.Precision.HIGHEST)[0]
    update = lax.all_gather(term, "smp", axis=0, tiled=True)
    start = lax.axis_index("smp") * rows
    return update, lax.dynamic_slice_in_dim(coeffs, start, rows, 0)


def solution(mesh):
    placed = (P("smp", "par"), P("smp", None), P("smp"))
    return jax.shard_map(
        body, mesh=mesh, in_specs=placed, out_specs=(P("par"), P("smp")), check_vma=False
    )
```

time: 1800 us -> 1110 us (0.62)
  other arithmetic: 637 us -> 15.5 us
  matrix products: 132 us -> 9.84 us
  local copies, waits for them, and re-layouts: 130 us -> 9.74 us
  Pallas kernels: 0 us -> 118 us
  waiting for transfers between devices: 790 us -> 871 us
    reduce_scatter x0 -> x1, waiting for transfers between devices: none -> 669 us  [body(): lax.psum_scatter(part, ('smp', 'par'), scatter_dimension=0, tiled=True)]
    another operation x70 -> x0, other arithmetic: 614 us -> none  [the longest x59 319 us: blocked_cholesky(): diag_factor = jnp.linalg.cholesky(diag_part)]
    all_gather x2 -> x1, waiting for transfers between devices: 645 us -> 202 us  [body(): gram = lax.all_gather(block, ('smp', 'par'), axis=0, tiled=True)]
    psum x1 -> x0, waiting for transfers between devices: 145 us -> none  [body(): row_block = lax.psum(partial_value, 'par')]
    pallas_call x0 -> x1, Pallas kernels: none -> 118 us  [solve(): pl.pallas_call(functools.partial(kernel, n), out_shape=jax.ShapeDtypeStru...]
    another operation x206 -> x0, local copies, waits for them, and re-layouts: 89.9 us -> none
    another operation x107 -> x0, matrix products: 88.7 us -> none  [the longest x62 51.5 us: body(): solved = jax.scipy.linalg.cho_solve((factor, True), eps)]
    psum x2 -> x0, blocking collectives: 55.1 us -> none  [the longest x1 28.7 us: body(): col_sum = lax.psum(jnp.sum(log_derivs.astype(jnp.float32), axis=0), 'smp')]
  transfers between devices with their start and end apart: 3 -> 2, of which waited for: 3 -> 2; matrix products, arithmetic and copies ran while one was open for 0% -> 0% of each run, Pallas kernels for 0% -> 0%
where the time goes in v1:
time: 1110 us; the launch traced here: 1100 us
  waiting for transfers between devices  871 us (78%)
  Pallas kernels  118 us (11%)
  blocking collectives  62.9 us (6%)
  other arithmetic  15.5 us (1%)
  between operations  14.8 us (1%)
    reduce_scatter x1, waiting for transfers between devices, body(): lax.psum_scatter(part, ('smp', 'par'), scatter_dimension=0, tiled=True)  669 us
    all_gather x1, waiting for transfers between devices, body(): gram = lax.all_gather(block, ('smp', 'par'), axis=0, tiled=True)  202 us
    pallas_call x1, Pallas kernels, solve(): pl.pallas_call(functools.partial(kernel, n), out_shape=jax.ShapeDtypeStru...  118 us
    all_to_all x1, blocking collectives, body(): lax.all_to_all(log_derivs, 'smp', split_axis=1, concat_axis=0, tiled=True)  32.1 us
  transfers between devices with their start and end apart: 2, of which 2 were waited for; matrix products, arithmetic and copies ran while one was open for 0% of the time, Pallas kernels for 0%

profile of v1, /device:TPU:1, one launch (start us, length us, event | category | flops | bytes accessed | tf_op | source)
XLA Modules:
  0.0 1101.9 jit_solution(5796325844484593573)
XLA Ops:
  7.2 0.0 reduce-scatter.2.cloned.1.call-start
  7.2 4.1 copy.7
  11.3 32.1 %all_to_all.13 = bf16[256,8,512]{0,2,1:T(8,128)(2,1)S(1)} all-to-all(bf16[256,8,512]{0,2,1:T(8,128)(2,1)} %bitcast.28), channel_id=1, replica_groups=mesh['smp'=8,'par'=16] {'smp'}, dimensions={1} | all-to-all | bytes 4194304 | tf_op jit(solution)/shard_map/all_to_all | solution.py:210
  43.4 0.4 convert_reduce_fusion
  43.8 1.9 fusion.2
  45.7 2.9 copy.8
  48.6 8.1 fusion.10
  56.7 0.0 copy-start
  56.7 0.0 copy-start.1
  56.7 0.0 reduce-scatter.2.cloned.1.call-update
  56.7 0.0 all-gather.4.cloned.1.call-start
  56.7 669.2 %reduce-scatter.2.cloned.1.call-done = f32[16,2048]{1,0:T(8,128)} async-done(((f32[2048,2048]{1,0:T(8,128)}), f32[16,2048]{1,0:T(8,128)}) %reduce-scatter.2.cloned.1.call-update) | async-done | bytes 131088 | tf_op jit(solution)/shard_map/reduce_scatter | solution.py:214
  725.9 0.0 all-gather.4.cloned.1.call-update
  725.9 0.0 copy-done
  726.2 0.1 maximum_add_fusion
  726.2 0.1 multiply_reduce_fusion.1
  726.3 0.0 copy-done.1
  726.3 11.8 %all-gather = f32[8,1,256]{2,1,0:T(1,128)S(1)} all-gather(f32[1,1,256]{2,1,0:T(1,128)S(1)} %bitcast.32), channel_id=1, replica_groups=mesh['smp'=8,'par'=16] {'smp'}, dimensions={0}, use_global_device_ids=true | all-gather | bytes 9216 | tf_op jit(solution)/shard_map/all_gather | solution.py:208
  738.1 0.6 reduce_sum.39
  739.4 0.7 scatter.4.e_ref
  740.0 201.8 %all-gather.4.cloned.1.call-done = f32[2048,2048]{1,0:T(8,128)} async-done(((f32[16,2048]{1,0:T(8,128)}), f32[2048,2048]{1,0:T(8,128)}) %all-gather.4.cloned.1.call-update) | async-done | bytes 16777232 | tf_op jit(solution)/shard_map/all_gather | solution.py:215
  941.8 12.4 %select_add_fusion.a_ref = f32[2048,2048]{1,0:T(8,128)} fusion(f32[2048,2048]{1,0:T(8,128)} %all-gather.4.cloned.1.call-done), kind=kLoop, calls=%fused_computation | loop fusion | flops 12582912 | bytes 33554432 | tf_op jit(solution)/shard_map/add | solution.py:216
  954.2 118.0 %shard_map.50 = f32[16,2048]{1,0:T(8,128)} custom-call(f32[2048,2048]{1,0:T(8,128)} %select_add_fusion.a_ref, f32[16,2048]{1,0:T(8,128)} %scatter.4.e_ref), custom_call_target="tpu_custom_call" | custom-call | tf_op jit(solution)/shard_map/pallas_call | solution.py:166
  1072.3 1.7 convolution_bitcast_fusion
  1074.0 0.9 slice.68
  1074.9 19.0 %all-gather.1 = f32[8,1,512]{2,1,0:T(1,128)S(1)} all-gather(f32[1,1,512]{2,1,0:T(1,128)S(1)} %convolution_bitcast_fusion), channel_id=1, replica_groups=mesh['smp'=8,'par'=16] {'smp'}, dimensions={0}, use_global_device_ids=true | all-gather | bytes 18432 | tf_op jit(solution)/shard_map/all_gather | solution.py:218
  1093.9 0.6 constant_dynamic-slice_fusion
  1094.5 0.6 copy.10
  (13 shorter events, 0.2 us)
Async XLA Ops:
  7.2 718.7 %reduce-scatter.2.cloned.1.call-start = ((), (), s32[]{:S(2)}) async-start(), calls=%async_computation.2 | async-start | bytes 16908288 | tf_op jit(solution)/shard_map/reduce_scatter | solution.py:214
  56.7 669.3 %copy-start = (s32[256,100]{0,1:T(8,128)S(1)}, s32[256,100]{0,1:T(8,128)}, u32[]{:S(2)}) copy-start(s32[256,100]{0,1:T(8,128)} %param.6) | copy-start | bytes 307204
  56.7 669.6 %copy-start.1 = (f32[256]{0:T(256)S(1)}, f32[256]{0:T(256)}, u32[]{:S(2)}) copy-start(f32[256]{0:T(256)} %param.7) | copy-start | bytes 3076
  56.7 885.1 %all-gather.4.cloned.1.call-start = ((), (), s32[]{:S(2)}) async-start(), calls=%async_computation.3 | async-start | bytes 16908288 | tf_op jit(solution)/shard_map/all_gather | solution.py:215
Sparse Core Ops, SparseCore 0:
  56.8 669.0 reduce-scatter.1
  727.6 214.1 all-gather.3

commit v2 on v1

--- a/solution.py
+++ b/solution.py
@@ -1,5 +1,6 @@
 import functools
 import jax, jax.numpy as jnp
+import numpy as np
 from jax import lax
 from jax.experimental import pallas as pl
 from jax.experimental.pallas import tpu as pltpu
@@ -87,8 +88,17 @@
         Wref[8 * g : 8 * g + 8, :] = jnp.where(lane <= sub + 8 * g, U[g], 0.0)
 
 
+def folded_tile(a_ref, nb, i, k):
+    upper = i >= nb // 2
+    a = jnp.where(upper, nb - 1 - i, i)
+    j = jnp.where(upper, k, nb - i + k)
+    return a_ref[pl.ds(pl.multiple_of(a * B, B), B), pl.ds(pl.multiple_of(j * B, B), B)]
+
+
 def kernel(n, a_ref, e_ref, x_ref, lhi, llo, c, ec, whi, wlo, D, W, T, R, z):
     nb = n // B
+    diag = lax.broadcasted_iota(jnp.int32, (H, H), 0) == lax.broadcasted_iota(jnp.int32, (H, H), 1)
+    damp = jnp.where(diag, jnp.float32(0.2), jnp.float32(0.0))
 
     def inner(k, _):
         rows_k = pl.ds(pl.multiple_of(k * B, B), B)
@@ -98,8 +108,11 @@
                 cols = slice(kk * B, kk * B + B)
                 w = kk * B
                 if kk == 0:
-                    c[...] = a_ref[:, cols]
                     ec[...] = e_ref[:, cols]
+
+                    @pl.loop(0, nb)
+                    def _(i):
+                        c[pl.ds(pl.multiple_of(i * B, B), B), :] = folded_tile(a_ref, nb, i, 0)
                 else:
                     bh, bl = lhi[w : w + B, :w], llo[w : w + B, :w]
                     eh, el = lhi[n : n + 16, :w], llo[n : n + 16, :w]
@@ -108,15 +121,15 @@
                     @pl.loop(kk, nb)
                     def _(i):
                         ri = pl.ds(pl.multiple_of(i * B, B), B)
-                        c[ri, :] = a_ref[ri, cols] - dot3(lhi[ri, :w], llo[ri, :w], bh, bl, NT)
+                        c[ri, :] = folded_tile(a_ref, nb, i, kk) - dot3(lhi[ri, :w], llo[ri, :w], bh, bl, NT)
 
         d0 = pl.multiple_of(k * B, B)
-        D[0] = c[pl.ds(d0, H), 0:H]
+        D[0] = c[pl.ds(d0, H), 0:H] + damp
         inverse_block_ref(D, W, T, R, 0)
         c21 = c[pl.ds(d0 + H, H), 0:H]
         W1 = W[0]
         l21 = mm(c21, W1, NT)
-        D[1] = c[pl.ds(d0 + H, H), H:B] - mm(l21, l21, NT)
+        D[1] = c[pl.ds(d0 + H, H), H:B] + damp - mm(l21, l21, NT)
         inverse_block_ref(D, W, T, R, 1)
         W2 = W[1]
         w21 = -mm(W2, mm(l21, W1, NN), NN)
@@ -159,7 +172,7 @@
 
 
 def solve(a, eps):
-    n = a.shape[0]
+    n = eps.shape[0]
     e = jnp.zeros((16, n), jnp.float32).at[0].set(eps)
     nb = n // B
     vm = pl.BlockSpec(memory_space=pltpu.VMEM)
@@ -183,7 +196,241 @@
         ],
         compiler_params=pltpu.CompilerParams(vmem_limit_bytes=60 * 2**20),
     )(a, e)
-    return x[0]
+    return x
+
+
+MESH = pl.DeviceIdType.MESH
+PORTIONS = 6
+STEPS = 6
+
+
+def place():
+    smp, par = lax.axis_index("smp"), lax.axis_index("par")
+    y, z_lo = lax.div(smp, 2), lax.rem(smp, 2)
+    x, z_hi, core = lax.div(par, 4), lax.rem(lax.div(par, 2), 2), lax.rem(par, 2)
+    return (x, y, z_hi * 2 + z_lo), core
+
+
+def device(pos, core):
+    x, y, z = pos
+    return (y * 2 + lax.rem(z, 2), x * 4 + lax.div(z, 2) * 2 + core)
+
+
+def plan(pos, core, q):
+    out = []
+    for stage in range(3):
+        axis = (q // 2 + stage) % 3
+        i = pos[axis]
+        low, high = lax.rem(i, 2), lax.div(i, 2)
+        near, far = i + 1 - 2 * low, 3 - i
+        if q % 2 == 0:
+            order = [(near, lax.rem(low + high, 2)), (far, high)]
+        else:
+            order = [(far, high), (near, low)]
+        for other, bit in order:
+            there = list(pos)
+            there[axis] = other
+            out.append((device(there, core), bit))
+    return out
+
+
+def remote(src, dst, send, recv, who):
+    return pltpu.make_async_remote_copy(
+        src_ref=src, dst_ref=dst, send_sem=send, recv_sem=recv, device_id=who, device_id_type=MESH
+    )
+
+
+def eight(x):
+    return pl.multiple_of(x, 8)
+
+
+def gram_kernel(total, x_ref, en_ref, O, xa, ebuf, F, recv, xp,
+                share_sem, rs_send, rs_recv, ag_send, ag_recv, co_send, co_recv, e_send, e_recv):
+    pos, core = place()
+    smp, par = lax.axis_index("smp"), lax.axis_index("par")
+    n, kp = x_ref.shape
+    nb = n // B
+    half = F.shape[0]
+    width = F.shape[1] // PORTIONS
+    plans = [plan(pos, core, q) for q in range(PORTIONS)]
+    partner = device(pos, 1 - core)
+    others = [(lax.rem(smp + d, 8), par) for d in range(1, 8)]
+    peers = [partner] + [plans[2 * a][s][0] for a in range(3) for s in range(2)] + others
+    barrier = pltpu.get_barrier_semaphore()
+    for who in peers:
+        pl.semaphore_signal(barrier, inc=1, device_id=who, device_id_type=MESH)
+
+    scale = 1.0 / np.sqrt(np.float32(total))
+
+    def add(i, acc):
+        r = pl.ds(pl.multiple_of(i * 64, 64), 64)
+        return acc + jnp.sum(x_ref[r, :].astype(jnp.float32).reshape(8, 8, kp), axis=0)
+
+    acc = lax.fori_loop(0, n // 64, add, jnp.zeros((8, kp), jnp.float32))
+    mean = jnp.sum(acc, axis=0, keepdims=True) / total
+
+    @pl.loop(0, n // 64)
+    def _(i):
+        r = pl.ds(pl.multiple_of(i * 64, 64), 64)
+        xa[r, :] = ((x_ref[r, :].astype(jnp.float32) - mean) * scale).astype(jnp.bfloat16)
+
+    ebuf[pl.ds(smp, 1)] = en_ref[...][None]
+    pl.semaphore_wait(barrier, len(peers))
+    share = remote(xa, xp, share_sem.at[0], share_sem.at[1], partner)
+    share.start()
+    spread = [remote(en_ref, ebuf.at[smp], e_send.at[d], e_recv.at[d], others[d]) for d in range(7)]
+    for copy in spread:
+        copy.start()
+
+    def tiles(src, first):
+        @pl.loop(0, 2 * (nb + 1))
+        def _(t):
+            a_local = lax.div(t, nb + 1)
+            j = lax.rem(t, nb + 1)
+            a = core * (nb // 4) + a_local
+            tall = j < nb - a
+            r = jnp.where(tall, nb - 1 - a, a)
+            cb = jnp.where(tall, j, j - (nb - a))
+            rows = src[pl.ds(pl.multiple_of(r * B, B), B), :]
+            cols = src[pl.ds(pl.multiple_of(cb * B, B), B), :]
+            got = lax.dot_general(rows, cols, (NT, ((), ())), preferred_element_type=jnp.float32)
+            at = (pl.ds(pl.multiple_of(a_local * B, B), B), pl.ds(pl.multiple_of(j * B, B), B))
+            F[at] = got if first else F[at] + got
+
+    tiles(xa, True)
+    share.wait_recv()
+    tiles(xp, False)
+
+    def cols(q):
+        return slice(q * width, q * width + width)
+
+    offs = [half - (half >> t) for t in range(STEPS)]
+    size = [half >> (t + 1) for t in range(STEPS)]
+    base = [[jnp.int32(0)] for q in range(PORTIONS)]
+
+    def halving(t, q):
+        who, bit = plans[q][t]
+        src = F.at[pl.ds(eight(base[q][t] + (1 - bit) * size[t]), size[t]), cols(q)]
+        return remote(src, recv.at[pl.ds(offs[t], size[t]), cols(q)], rs_send.at[t, q], rs_recv.at[t, q], who)
+
+    def accumulate(t, q, start, rows):
+        at = (pl.ds(eight(base[q][t + 1] + start), rows), cols(q))
+        F[at] += recv[pl.ds(eight(offs[t] + start), rows), cols(q)]
+
+    copies = {}
+    for q in range(PORTIONS):
+        copies[0, q] = halving(0, q)
+        copies[0, q].start()
+    for t in range(STEPS):
+        for q in range(PORTIONS):
+            copies[t, q].wait_recv()
+            base[q].append(base[q][t] + plans[q][t][1] * size[t])
+            if t + 1 < STEPS:
+                bit, s = plans[q][t + 1][1], size[t + 1]
+                accumulate(t, q, (1 - bit) * s, s)
+                copies[t + 1, q] = halving(t + 1, q)
+                copies[t + 1, q].start()
+                accumulate(t, q, bit * s, s)
+            else:
+                accumulate(t, q, 0, size[t])
+
+    def region(row, rows, q):
+        return O.at[pl.ds(eight(core * half + row), rows), cols(q)]
+
+    def doubling(t, q):
+        here = region(base[q][t + 1], size[t], q)
+        return remote(here, here, ag_send.at[t, q], ag_recv.at[t, q], plans[q][t][0])
+
+    def across(t, q, row, rows):
+        here = region(row, rows, q)
+        return remote(here, here, co_send.at[t, q], co_recv.at[t, q], partner)
+
+    back, forth = {}, []
+    for q in range(PORTIONS):
+        row, rows = base[q][STEPS], size[STEPS - 1]
+        O[pl.ds(eight(core * half + row), rows), cols(q)] = F[pl.ds(eight(row), rows), cols(q)]
+        back[STEPS - 1, q] = doubling(STEPS - 1, q)
+        back[STEPS - 1, q].start()
+        forth.append(across(STEPS, q, row, rows))
+        forth[-1].start()
+    for t in range(STEPS - 1, -1, -1):
+        for q in range(PORTIONS):
+            back[t, q].wait_recv()
+            if t > 0:
+                back[t - 1, q] = doubling(t - 1, q)
+                back[t - 1, q].start()
+            forth.append(across(t, q, base[q][t] + (1 - plans[q][t][1]) * size[t], size[t]))
+            forth[-1].start()
+    share.wait_send()
+    for copy in spread:
+        copy.wait()
+    for copy in [*copies.values(), *back.values()]:
+        copy.wait_send()
+    for copy in forth:
+        copy.wait()
+
+
+def damped_gram(mine, energy, total):
+    n, kp = mine.shape
+    nb = n // B
+    wide = (nb + 1) * B
+    vm = pl.BlockSpec(memory_space=pltpu.VMEM)
+    dma = pltpu.SemaphoreType.DMA
+    grid = (STEPS, PORTIONS)
+    return pl.pallas_call(
+        functools.partial(gram_kernel, total),
+        out_shape=[
+            jax.ShapeDtypeStruct((n // 2, wide), jnp.float32),
+            jax.ShapeDtypeStruct((n, kp), jnp.bfloat16),
+            jax.ShapeDtypeStruct((8, 8, 128), jnp.float32),
+        ],
+        in_specs=[vm, vm],
+        out_specs=[vm, vm, vm],
+        scratch_shapes=[
+            pltpu.VMEM((n // 4, wide), jnp.float32),
+            pltpu.VMEM((n // 4, wide), jnp.float32),
+            pltpu.VMEM((n, kp), jnp.bfloat16),
+            dma((2,)), dma(grid), dma(grid), dma(grid), dma(grid),
+            dma((STEPS + 1, PORTIONS)), dma((STEPS + 1, PORTIONS)), dma((7,)), dma((7,)),
+        ],
+        compiler_params=pltpu.CompilerParams(
+            vmem_limit_bytes=48 * 2**20, collective_id=1, has_side_effects=True
+        ),
+    )(mine, energy)
+
+
+def update_kernel(x_ref, xc_ref, u_ref, send, recv):
+    smp, par = lax.axis_index("smp"), lax.axis_index("par")
+    others = [(lax.rem(smp + d, 8), par) for d in range(1, 8)]
+    barrier = pltpu.get_barrier_semaphore()
+    for who in others:
+        pl.semaphore_signal(barrier, inc=1, device_id=who, device_id_type=MESH)
+    hi, lo = split(x_ref[...])
+    d = lambda a: lax.dot_general(a, xc_ref[...], (NN, ((), ())), preferred_element_type=jnp.float32)
+    term = (d(hi) + d(lo))[0:8]
+    u_ref[pl.ds(smp, 1)] = term[None]
+    pl.semaphore_wait(barrier, len(others))
+    here = u_ref.at[smp]
+    copies = [remote(here, here, send.at[i], recv.at[i], others[i]) for i in range(7)]
+    for copy in copies:
+        copy.start()
+    for copy in copies:
+        copy.wait()
+
+
+def project(x, xc):
+    vm = pl.BlockSpec(memory_space=pltpu.VMEM)
+    u = pl.pallas_call(
+        update_kernel,
+        out_shape=jax.ShapeDtypeStruct((8, 8, xc.shape[1]), jnp.float32),
+        in_specs=[vm, vm],
+        out_specs=vm,
+        scratch_shapes=[pltpu.SemaphoreType.DMA((7,)), pltpu.SemaphoreType.DMA((7,))],
+        compiler_params=pltpu.CompilerParams(
+            vmem_limit_bytes=32 * 2**20, collective_id=2, has_side_effects=True
+        ),
+    )(x, xc)
+    return u[:, 0, :].reshape(-1)
 
 
 SIDE = 10
@@ -202,22 +449,18 @@
 
 def body(log_derivs, spins, hop_energy):
     rows = log_derivs.shape[0]
-    total = rows * lax.axis_size("smp")
+    total = rows * 8
     scale = 1.0 / jnp.sqrt(jnp.float32(total))
     energy = local_energy(spins) + hop_energy
-    all_energy = lax.all_gather(energy, "smp", axis=0, tiled=True)
+    energy = jnp.pad(energy.reshape(rows // 128, 128), ((0, 8 - rows // 128), (0, 0)))
+    mine = lax.all_to_all(log_derivs, "smp", split_axis=1, concat_axis=0, tiled=True)
+    gram, centered, energies = damped_gram(mine, energy, total)
+    all_energy = energies[:, : rows // 128].reshape(-1)
     eps = (all_energy - jnp.mean(all_energy)) * scale
-    mine = lax.all_to_all(log_derivs, "smp", split_axis=1, concat_axis=0, tiled=True)
-    wide = mine.astype(jnp.float32)
-    centered = ((wide - jnp.sum(wide, axis=0) / total) * scale).astype(jnp.bfloat16)
-    part = lax.dot_general(centered, centered, (NT, ((), ())), preferred_element_type=jnp.float32)
-    block = lax.psum_scatter(part, ("smp", "par"), scatter_dimension=0, tiled=True)
-    gram = lax.all_gather(block, ("smp", "par"), axis=0, tiled=True)
-    coeffs = solve(gram + 0.2 * jnp.eye(total, dtype=jnp.float32), eps)
-    term = jnp.dot(coeffs[None], centered.astype(jnp.float32), precision=lax.Precision.HIGHEST)[0]
-    update = lax.all_gather(term, "smp", axis=0, tiled=True)
+    coeffs = solve(gram, eps)
+    update = project(coeffs, centered)
     start = lax.axis_index("smp") * rows
-    return update, lax.dynamic_slice_in_dim(coeffs, start, rows, 0)
+    return update, lax.dynamic_slice_in_dim(coeffs[0], start, rows, 0)
 
 
 def solution(mesh):

time: 1110 us -> 251 us (0.23)
  waiting for transfers between devices: 871 us -> 29.8 us
  Pallas kernels: 118 us -> 205 us
  blocking collectives: 62.9 us -> 0 us
  other arithmetic: 15.5 us -> 0.81 us
  between operations: 14.8 us -> 1.42 us
    reduce_scatter x1 -> x0, waiting for transfers between devices: 669 us -> none  [body(): lax.psum_scatter(part, ('smp', 'par'), scatter_dimension=0, tiled=True)]
    all_gather x1 -> x0, waiting for transfers between devices: 202 us -> none  [body(): gram = lax.all_gather(block, ('smp', 'par'), axis=0, tiled=True)]
    pallas_call x0 -> x2, Pallas kernels: none -> 88.2 us  [the longest x1 82.7 us: damped_gram(): pl.pallas_call(functools.partial(gram_kernel, total), out_shape=[jax.Shap...]
    all_to_all x1 -> x0, blocking collectives: 32.1 us -> none  [body(): lax.all_to_all(log_derivs, 'smp', split_axis=1, concat_axis=0, tiled=True)]
    all_gather x2 -> x0, blocking collectives: 30.8 us -> none  [the longest x1 19 us: body(): update = lax.all_gather(term, 'smp', axis=0, tiled=True)]
    all_to_all x0 -> x1, waiting for transfers between devices: none -> 29.8 us  [body(): lax.all_to_all(log_derivs, 'smp', split_axis=1, concat_axis=0, tiled=True)]
    add x2 -> x0, other arithmetic: 12.4 us -> none  [the longest x1 12.4 us: body(): coeffs = solve(gram + 0.2 * jnp.eye(total, dtype=jnp.float32), eps)]
  transfers between devices with their start and end apart: 2 -> 1, of which waited for: 2 -> 1; matrix products, arithmetic and copies ran while one was open for 0% -> 0% of each run, Pallas kernels for 0% -> 0%
where the time goes in v2:
time: 251 us
  Pallas kernels  205 us (82%)
  waiting for transfers between devices  29.8 us (12%)
  local copies, waits for them, and re-layouts  7.63 us (3%)
  starting transfers between devices  6.51 us (3%)
    pallas_call x1, Pallas kernels, solve(): pl.pallas_call(functools.partial(kernel, n), out_shape=jax.ShapeDtypeStru...  116 us
    pallas_call x1, Pallas kernels, damped_gram(): pl.pallas_call(functools.partial(gram_kernel, total), out_shape=[jax.Shap...  82.7 us
    all_to_all x1, waiting for transfers between devices, body(): lax.all_to_all(log_derivs, 'smp', split_axis=1, concat_axis=0, tiled=True)  29.8 us
    all_to_all x1, starting transfers between devices, body(): lax.all_to_all(log_derivs, 'smp', split_axis=1, concat_axis=0, tiled=True)  6.51 us
    pallas_call x1, Pallas kernels, project(): pl.pallas_call(update_kernel, out_shape=jax.ShapeDtypeStruct((8, 8, xc.sh...  5.52 us
  transfers between devices with their start and end apart: 1, of which 1 were waited for; matrix products, arithmetic and copies ran while one was open for 0% of the time, Pallas kernels for 0%

profile of v2, /device:TPU:1, one launch (start us, length us, event | category | flops | bytes accessed | tf_op | source)
XLA Modules:
  0.0 250.7 jit_solution(17734255781882058613)
XLA Ops:
  0.6 3.1 %copy.8 = bf16[32,8,8,512]{3,2,0,1:T(8,128)(2,1)} copy(bf16[32,8,8,512]{3,2,1,0:T(8,128)(2,1)} %bitcast.21) | data formatting | bytes 4194304 | tf_op jit(solution)/shard_map/all_to_all | solution.py:456
  3.7 0.0 copy-start.3
  3.8 6.5 %all-to-all-start = ((bf16[256,8,512]{2,0,1:T(8,128)(2,1)}), bf16[256,8,512]{2,0,1:T(8,128)(2,1)S(1)}, u32[]{:S(2)}, u32[]{:S(2)}) async-start(bf16[256,8,512]{2,0,1:T(8,128)(2,1)} %bitcast.20), calls=%async_computation | async-start | bytes 4194304 | tf_op jit(solution)/shard_map/all_to_all | solution.py:456
  10.3 0.0 copy-done.3
  10.3 0.0 copy-start.4
  10.4 0.1 maximum_add_fusion
  10.6 0.1 multiply_reduce_fusion.1
  10.6 0.3 copy-done.4
  11.0 29.8 %all-to-all-done = bf16[256,8,512]{2,0,1:T(8,128)(2,1)S(1)} async-done(((bf16[256,8,512]{2,0,1:T(8,128)(2,1)}), bf16[256,8,512]{2,0,1:T(8,128)(2,1)S(1)}, u32[]{:S(2)}, u32[]{:S(2)}) %all-to-all-start) | async-done | bytes 2097184 | tf_op jit(solution)/shard_map/all_to_all | solution.py:456
  40.8 82.7 %shard_map.50 = (f32[1024,2304]{1,0:T(8,128)}, bf16[2048,512]{1,0:T(8,128)(2,1)S(1)}, f32[8,8,128]{2,1,0:T(8,128)S(1)}) custom-call(bf16[2048,512]{1,0:T(8,128)(2,1)S(1)} %bitcast.19, f32[8,128]{1,0:T(8,128)S(1)} %pad.7.en_ref), custom_call_target="tpu_custom_call" | custom-call | tf_op jit(solution)/shard_map/pallas_call | solution.py:380
  123.4 0.0 copy-start
  123.4 1.3 copy-done
  124.7 0.6 slice_reduce_fusion
  126.0 0.7 scatter.4.e_ref
  126.7 0.0 copy-start.1
  126.7 116.3 %shard_map.51.x_ref = f32[16,2048]{1,0:T(8,128)} custom-call(f32[1024,2304]{1,0:T(8,128)} %get-tuple-element.17.a_ref, f32[16,2048]{1,0:T(8,128)} %scatter.4.e_ref), custom_call_target="tpu_custom_call" | custom-call | tf_op jit(solution)/shard_map/pallas_call | solution.py:179
  243.0 0.0 slice-start
  243.0 0.0 copy-done.1
  243.0 0.0 copy-start.2
  243.0 1.0 copy-done.2
  244.0 5.5 %shard_map.52 = f32[8,8,512]{2,1,0:T(8,128)S(1)} custom-call(f32[16,2048]{1,0:T(8,128)S(1)} %copy-done.2, bf16[2048,512]{1,0:T(8,128)(2,1)S(1)} %copy-done.1), custom_call_target="tpu_custom_call" | custom-call | tf_op jit(solution)/shard_map/pallas_call | solution.py:423
  249.5 0.6 slice.62
  250.1 0.0 slice-done
  250.1 0.6 constant_dynamic-slice_fusion
  (13 shorter events, 0.2 us)
Async XLA Ops:
  3.7 6.5 %copy-start.3 = (s32[256,100]{0,1:T(8,128)S(1)}, s32[256,100]{0,1:T(8,128)}, u32[]{:S(2)}) copy-start(s32[256,100]{0,1:T(8,128)} %param.6) | copy-start | bytes 307204
  3.8 37.0 %all-to-all-start = ((bf16[256,8,512]{2,0,1:T(8,128)(2,1)}), bf16[256,8,512]{2,0,1:T(8,128)(2,1)S(1)}, u32[]{:S(2)}, u32[]{:S(2)}) async-start(bf16[256,8,512]{2,0,1:T(8,128)(2,1)} %bitcast.20), calls=%async_computation | async-start | bytes 4194304 | tf_op jit(solution)/shard_map/all_to_all | solution.py:456
  10.3 0.7 copy-start.4
  123.4 1.3 copy-start
  126.7 116.3 %copy-start.1 = (bf16[2048,512]{1,0:T(8,128)(2,1)S(1)}, bf16[2048,512]{1,0:T(8,128)(2,1)}, u32[]{:S(2)}) copy-start(bf16[2048,512]{1,0:T(8,128)(2,1)} %copy-done) | copy-start | bytes 6291460
  243.0 7.1 %slice-start = ((f32[16,2048]{1,0:T(8,128)}), f32[1,2048]{1,0:T(1,128)S(1)}, s32[]{:S(2)}) async-start(f32[16,2048]{1,0:T(8,128)} %shard_map.51.x_ref), calls=%async_computation.1 | async-start | bytes 16384 | tf_op jit(solution)/shard_map/slice | solution.py:463
  243.0 1.0 copy-start.2

commit v3 on v2

--- a/solution.py
+++ b/solution.py
@@ -8,6 +8,8 @@
 
 B = 256
 H = 128
+NT = ((1,), (1,))
+NN = ((1,), (0,))
 
 
 def split(x):
@@ -20,143 +22,174 @@
     return d(ah, bh) + (d(ah, bl) + d(al, bh))
 
 
-NT = ((1,), (1,))
-NN = ((1,), (0,))
-
-
-def mm(a, b, dims):
-    return dot3(*split(a), *split(b), dims)
-
-
-def recip(x):
-    r = pl.reciprocal(x, approx=True)
-    return r * (2.0 - x * r)
-
-
-def factor_inverse(S, T, R):
+def splat(x):
+    return jnp.broadcast_to(x, (8, H))
+
+
+def factor_inverse(groups, T, R, A2, beside):
     lane = lax.broadcasted_iota(jnp.int32, (8, H), 1)
     sub = lax.broadcasted_iota(jnp.int32, (8, H), 0)
     out = []
-    groups = list(S)
+    corner = [splat(groups[0][:, j : j + 1]) for j in range(8)]
     for p in range(16):
-        rows = groups[p]
-        lo = 8 * p
+        if beside is not None:
+            beside(p)
+        lo, slot = 8 * p, p % 2
+        pivots, at = groups[p], 64 * slot
         for j in range(8):
-            T[8 * j : 8 * j + 8, :] = jnp.broadcast_to(rows[:, lo + j : lo + j + 1], (8, H))
-        indiag = (lane >= lo) & (lane < lo + 8)
-        Pi = jnp.where(indiag, (lane - lo == sub).astype(jnp.float32), rows)
-        R[...] = Pi
+            T[at + 8 * j : at + 8 * j + 8, :] = corner[j]
+        inside = (lane >= lo) & (lane < lo + 8)
+        R[8 * slot : 8 * slot + 8, :] = jnp.where(inside, (lane - lo == sub).astype(jnp.float32), pivots)
         e = {}
         for j in range(8):
             for i in range(j, 8):
-                e[i, j] = jnp.broadcast_to(T[8 * j + i : 8 * j + i + 1, :], (8, H))
-        Y = [jnp.broadcast_to(R[i : i + 1, :], (8, H)) for i in range(8)]
-        m, r, U = {}, [], None
+                e[i, j] = splat(T[at + 8 * j + i : at + 8 * j + i + 1, :])
+        y = [splat(R[8 * slot + i : 8 * slot + i + 1, :]) for i in range(8)]
+        last = p == 15
+        if not last:
+            near = groups[p + 1]
+            a = [splat(near[:, lo + j : lo + j + 1]) for j in range(8)]
+            corner = [splat(near[:, lo + 8 + j : lo + 9 + j]) for j in range(8)]
+            near = jnp.where(inside, 0.0, near)
+        m, r, u = {}, [], None
         for k in range(8):
-            rk = recip(e[k, k])
+            rk = pl.reciprocal(e[k, k], approx=True)
             r.append(rk)
             for i in range(k + 1, 8):
                 m[i, k] = e[i, k] * rk
             for i in range(k + 1, 8):
                 for q in range(k + 1, i + 1):
-                    e[i, q] = e[i, q] - m[i, k] * e[q, k]
+                    if i == q == k + 1:
+                        e[i, q] = e[i, q] - (e[i, k] * e[i, k]) * rk
+                    else:
+                        e[i, q] = e[i, q] - m[i, k] * e[q, k]
             for i in range(k + 1, 8):
-                Y[i] = Y[i] - m[i, k] * Y[k]
-            Uk = Y[k] * lax.rsqrt(e[k, k])
-            U = Uk if k == 0 else jnp.where(sub == k, Uk, U)
-        out.append(U)
-        V = [None] * 8
+                y[i] = y[i] - m[i, k] * y[k]
+            row = y[k] * lax.rsqrt(e[k, k])
+            u = row if k == 0 else jnp.where(sub == k, row, u)
+            if not last:
+                for i in range(k + 1, 8):
+                    a[i] = a[i] - m[i, k] * a[k]
+                scaled = a[k] * rk
+                A2[at + 8 * k : at + 8 * k + 8, :] = scaled
+                near = near - scaled * y[k]
+                for j in range(8):
+                    corner[j] = corner[j] - a[k] * splat(A2[at + 8 * k + j : at + 8 * k + j + 1, :])
+        out.append(u)
+        if last:
+            break
+        groups[p + 1] = near
+        v = [None] * 8
         for j in range(7, -1, -1):
-            v = r[j] * Y[j]
+            t = r[j] * y[j]
             for k in range(7, j, -1):
-                v = v - m[k, j] * V[k]
-            V[j] = v
-        for g in range(p + 1, 16):
+                t = t - m[k, j] * v[k]
+            v[j] = t
+        for g in range(p + 2, 16):
             old = groups[g]
-            base = jnp.where(indiag, 0.0, old)
-            terms = [jnp.broadcast_to(old[:, lo + j : lo + j + 1], (8, H)) * V[j] for j in range(8)]
-            t = ((terms[0] + terms[1]) + (terms[2] + terms[3])) + ((terms[4] + terms[5]) + (terms[6] + terms[7]))
-            groups[g] = base - t
-    return out
-
-
-def inverse_block(D, Wref, T, R):
-    U = factor_inverse([D[8 * g : 8 * g + 8, :] for g in range(16)], T, R)
-    lane = lax.broadcasted_iota(jnp.int32, (8, H), 1)
-    sub = lax.broadcasted_iota(jnp.int32, (8, H), 0)
-    for g in range(16):
-        Wref[8 * g : 8 * g + 8, :] = jnp.where(lane <= sub + 8 * g, U[g], 0.0)
-
-
-def folded_tile(a_ref, nb, i, k):
+            t = [splat(old[:, lo + j : lo + j + 1]) * v[j] for j in range(8)]
+            t = ((t[0] + t[1]) + (t[2] + t[3])) + ((t[4] + t[5]) + (t[6] + t[7]))
+            groups[g] = jnp.where(inside, 0.0, old) - t
+    return [jnp.where(lane <= sub + 8 * g, out[g], 0.0) for g in range(16)]
+
+
+def tile(nb, i, k):
     upper = i >= nb // 2
     a = jnp.where(upper, nb - 1 - i, i)
     j = jnp.where(upper, k, nb - i + k)
-    return a_ref[pl.ds(pl.multiple_of(a * B, B), B), pl.ds(pl.multiple_of(j * B, B), B)]
-
-
-def kernel(n, a_ref, e_ref, x_ref, lhi, llo, c, ec, whi, wlo, D, W, T, R, z):
+    return pl.ds(pl.multiple_of(a * B, B), B), pl.ds(pl.multiple_of(j * B, B), B)
+
+
+def block(i):
+    return pl.ds(pl.multiple_of(i * B, B), B)
+
+
+SLOTS = 8
+
+
+def kernel(n, g_ref, e_ref, x_ref, G, lhi, llo, ec, whi, wlo, D, W, T, R, A2, z, sem):
     nb = n // B
+    load = pltpu.make_async_copy(g_ref, G.at[0 : n // 2, :], sem)
+    load.start()
+    ec[...] = e_ref[...]
     diag = lax.broadcasted_iota(jnp.int32, (H, H), 0) == lax.broadcasted_iota(jnp.int32, (H, H), 1)
     damp = jnp.where(diag, jnp.float32(0.2), jnp.float32(0.0))
-
-    def inner(k, _):
-        rows_k = pl.ds(pl.multiple_of(k * B, B), B)
-        for kk in range(nb):
-            @pl.when(k == kk)
-            def _():
-                cols = slice(kk * B, kk * B + B)
-                w = kk * B
-                if kk == 0:
-                    ec[...] = e_ref[:, cols]
-
-                    @pl.loop(0, nb)
-                    def _(i):
-                        c[pl.ds(pl.multiple_of(i * B, B), B), :] = folded_tile(a_ref, nb, i, 0)
-                else:
-                    bh, bl = lhi[w : w + B, :w], llo[w : w + B, :w]
-                    eh, el = lhi[n : n + 16, :w], llo[n : n + 16, :w]
-                    ec[...] = e_ref[:, cols] - dot3(eh, el, bh, bl, NT)
-
-                    @pl.loop(kk, nb)
-                    def _(i):
-                        ri = pl.ds(pl.multiple_of(i * B, B), B)
-                        c[ri, :] = folded_tile(a_ref, nb, i, kk) - dot3(lhi[ri, :w], llo[ri, :w], bh, bl, NT)
-
-        d0 = pl.multiple_of(k * B, B)
-        D[0] = c[pl.ds(d0, H), 0:H] + damp
-        inverse_block_ref(D, W, T, R, 0)
-        c21 = c[pl.ds(d0 + H, H), 0:H]
-        W1 = W[0]
-        l21 = mm(c21, W1, NT)
-        D[1] = c[pl.ds(d0 + H, H), H:B] + damp - mm(l21, l21, NT)
-        inverse_block_ref(D, W, T, R, 1)
-        W2 = W[1]
-        w21 = -mm(W2, mm(l21, W1, NN), NN)
-        zero = jnp.zeros((H, H), jnp.float32)
-        full = jnp.concatenate(
-            [jnp.concatenate([W1, zero], 1), jnp.concatenate([w21, W2], 1)], 0
-        )
-        wh, wl = split(full)
-        whi[k], wlo[k] = wh, wl
-        for kk in range(nb):
-            @pl.when(k == kk)
-            def _():
-                cols = slice(kk * B, kk * B + B)
-
-                @pl.loop(kk + 1, nb)
-                def _(i):
-                    ri = pl.ds(pl.multiple_of(i * B, B), B)
-                    ch, cl = split(c[ri, :])
-                    lhi[ri, cols], llo[ri, cols] = split(dot3(ch, cl, wh, wl, NT))
-
-                eh, el = split(ec[...])
-                y = dot3(eh, el, wh, wl, NT)
-                lhi[n : n + 16, cols], llo[n : n + 16, cols] = split(y)
-                z[:, cols] = y
+    load.wait()
+
+    def triangle(k, i):
+        ch, cl = split(G[tile(nb, i, k)])
+        th, tl = split(dot3(ch, cl, whi[k], wlo[k], NT))
+        lhi[block(i), block(k)], llo[block(i), block(k)] = th, tl
+        yh, yl = split(z[:, block(k)])
+        ec[:, block(i)] -= dot3(yh, yl, th, tl, NT)
+        return th, tl
+
+    def factor(k, h, slots):
+        def beside(p):
+            if p % (16 // SLOTS) != 0:
+                return
+            s = h * SLOTS + p // (16 // SLOTS)
+            live = s < (k + 1) * (nb - 1 - k)
+            i = jnp.minimum(k + 1 + lax.div(s, k + 1), nb - 1)
+            u = lax.rem(s, k + 1)
+            own = u == k
+            column = jnp.where(own, k, jnp.minimum(k + 1, nb - 1))
+            j = jnp.where(own, k - 1, u)
+            rows, cols = tile(nb, i, column)
+            rows = pl.ds(pl.multiple_of(jnp.where(live, rows.start, n // 2), B), B)
+            G[rows, cols] -= dot3(
+                lhi[block(i), block(j)], llo[block(i), block(j)],
+                lhi[block(column), block(j)], llo[block(column), block(j)], NT)
+
+        got = factor_inverse([D[8 * g : 8 * g + 8, :] for g in range(16)], T, R, A2, beside if slots else None)
+        for g in range(16):
+            W[h, 8 * g : 8 * g + 8, :] = got[g]
+
+    def chain(k, h):
+        some = (k > 0) & (k < nb - 1)
+
+        @pl.when(some)
+        def _():
+            factor(k, h, True)
+
+        @pl.when(jnp.logical_not(some))
+        def _():
+            factor(k, h, False)
+
+    def panel(k, _):
+        rows, cols = tile(nb, k, k)
+        r0, c0 = rows.start, cols.start
+
+        @pl.when(k > 0)
+        def _():
+            th, tl = triangle(k - 1, k)
+            G[rows, cols] -= dot3(th, tl, th, tl, NT)
+
+            @pl.loop(k + 1, nb)
+            def _(i):
+                triangle(k - 1, i)
+
+        top, low = pl.ds(r0, H), pl.ds(pl.multiple_of(r0 + H, H), H)
+        left, right = pl.ds(c0, H), pl.ds(pl.multiple_of(c0 + H, H), H)
+        D[...] = G[top, left] + damp
+        chain(k, 0)
+        w1h, w1l = split(W[0])
+        ah, al = split(G[low, left])
+        lh, ll = split(dot3(ah, al, w1h, w1l, NT))
+        D[...] = G[low, right] + damp - dot3(lh, ll, lh, ll, NT)
+        th, tl = split(dot3(lh, ll, w1h, w1l, NN))
+        whi[k, 0:H, 0:H], wlo[k, 0:H, 0:H] = w1h, w1l
+        whi[k, 0:H, H:B] = jnp.zeros((H, H), jnp.bfloat16)
+        wlo[k, 0:H, H:B] = jnp.zeros((H, H), jnp.bfloat16)
+        chain(k, 1)
+        w2h, w2l = split(W[1])
+        whi[k, H:B, H:B], wlo[k, H:B, H:B] = w2h, w2l
+        whi[k, H:B, 0:H], wlo[k, H:B, 0:H] = split(-dot3(w2h, w2l, th, tl, NN))
+        eh, el = split(ec[:, block(k)])
+        z[:, block(k)] = dot3(eh, el, whi[k], wlo[k], NT)
         return 0
 
-    lax.fori_loop(0, nb, inner, 0)
+    lax.fori_loop(0, nb, panel, 0)
     for kk in range(nb - 1, -1, -1):
         cols = slice(kk * B, kk * B + B)
         zh, zl = split(z[:, cols])
@@ -167,36 +200,33 @@
             z[:, : kk * B] -= dot3(xh, xl, lhi[cols, : kk * B], llo[cols, : kk * B], NN)
 
 
-def inverse_block_ref(D, W, T, R, h):
-    inverse_block(D[h], W.at[h], T, R)
-
-
 def solve(a, eps):
     n = eps.shape[0]
     e = jnp.zeros((16, n), jnp.float32).at[0].set(eps)
     nb = n // B
     vm = pl.BlockSpec(memory_space=pltpu.VMEM)
-    x = pl.pallas_call(
+    return pl.pallas_call(
         functools.partial(kernel, n),
         out_shape=jax.ShapeDtypeStruct((16, n), jnp.float32),
-        in_specs=[vm, vm],
+        in_specs=[pl.BlockSpec(memory_space=pl.ANY), vm],
         out_specs=vm,
         scratch_shapes=[
-            pltpu.VMEM((n + 16, n), jnp.bfloat16),
-            pltpu.VMEM((n + 16, n), jnp.bfloat16),
-            pltpu.VMEM((n, B), jnp.float32),
-            pltpu.VMEM((16, B), jnp.float32),
+            pltpu.VMEM((n // 2 + B, (nb + 1) * B), jnp.float32),
+            pltpu.VMEM((n, n), jnp.bfloat16),
+            pltpu.VMEM((n, n), jnp.bfloat16),
+            pltpu.VMEM((16, n), jnp.float32),
             pltpu.VMEM((nb, B, B), jnp.bfloat16),
             pltpu.VMEM((nb, B, B), jnp.bfloat16),
+            pltpu.VMEM((H, H), jnp.float32),
             pltpu.VMEM((2, H, H), jnp.float32),
-            pltpu.VMEM((2, H, H), jnp.float32),
-            pltpu.VMEM((64, H), jnp.float32),
-            pltpu.VMEM((8, H), jnp.float32),
+            pltpu.VMEM((128, H), jnp.float32),
+            pltpu.VMEM((16, H), jnp.float32),
+            pltpu.VMEM((128, H), jnp.float32),
             pltpu.VMEM((16, n), jnp.float32),
+            pltpu.SemaphoreType.DMA,
         ],
-        compiler_params=pltpu.CompilerParams(vmem_limit_bytes=60 * 2**20),
+        compiler_params=pltpu.CompilerParams(vmem_limit_bytes=56 * 2**20),
     )(a, e)
-    return x
 
 
 MESH = pl.DeviceIdType.MESH

time: 251 us -> 216 us (0.86)
  Pallas kernels: 205 us -> 170 us
    pallas_call x1, Pallas kernels: 116 us -> 81.8 us  [solve(): pl.pallas_call(functools.partial(kernel, n), out_shape=jax.ShapeDtypeStru...]
where the time goes in v3:
time: 216 us
  Pallas kernels  170 us (79%)
  waiting for transfers between devices  29.8 us (14%)
  local copies, waits for them, and re-layouts  7.61 us (4%)
  starting transfers between devices  6.51 us (3%)
    pallas_call x1, Pallas kernels, damped_gram(): pl.pallas_call(functools.partial(gram_kernel, total), out_shape=[jax.Shap...  82.7 us
    pallas_call x1, Pallas kernels, solve(): pl.pallas_call(functools.partial(kernel, n), out_shape=jax.ShapeDtypeStru...  81.8 us
    all_to_all x1, waiting for transfers between devices, body(): lax.all_to_all(log_derivs, 'smp', split_axis=1, concat_axis=0, tiled=True)  29.8 us
    all_to_all x1, starting transfers between devices, body(): lax.all_to_all(log_derivs, 'smp', split_axis=1, concat_axis=0, tiled=True)  6.51 us
    pallas_call x1, Pallas kernels, project(): pl.pallas_call(update_kernel, out_shape=jax.ShapeDtypeStruct((8, 8, xc.sh...  5.52 us
  transfers between devices with their start and end apart: 1, of which 1 were waited for; matrix products, arithmetic and copies ran while one was open for 0% of the time, Pallas kernels for 0%

profile of v3, /device:TPU:1, one launch (start us, length us, event | category | flops | bytes accessed | tf_op | source)
XLA Modules:
  0.0 216.2 jit_solution(3233544505934240901)
XLA Ops:
  0.6 3.1 %copy.8 = bf16[32,8,8,512]{3,2,0,1:T(8,128)(2,1)} copy(bf16[32,8,8,512]{3,2,1,0:T(8,128)(2,1)} %bitcast.21) | data formatting | bytes 4194304 | tf_op jit(solution)/shard_map/all_to_all | solution.py:486
  3.7 0.0 copy-start.3
  3.8 6.5 %all-to-all-start = ((bf16[256,8,512]{2,0,1:T(8,128)(2,1)}), bf16[256,8,512]{2,0,1:T(8,128)(2,1)S(1)}, u32[]{:S(2)}, u32[]{:S(2)}) async-start(bf16[256,8,512]{2,0,1:T(8,128)(2,1)} %bitcast.20), calls=%async_computation | async-start | bytes 4194304 | tf_op jit(solution)/shard_map/all_to_all | solution.py:486
  10.3 0.0 copy-done.3
  10.3 0.0 copy-start.4
  10.4 0.1 maximum_add_fusion
  10.6 0.1 multiply_reduce_fusion.1
  10.6 0.3 copy-done.4
  11.0 29.8 %all-to-all-done = bf16[256,8,512]{2,0,1:T(8,128)(2,1)S(1)} async-done(((bf16[256,8,512]{2,0,1:T(8,128)(2,1)}), bf16[256,8,512]{2,0,1:T(8,128)(2,1)S(1)}, u32[]{:S(2)}, u32[]{:S(2)}) %all-to-all-start) | async-done | bytes 2097184 | tf_op jit(solution)/shard_map/all_to_all | solution.py:486
  40.8 82.7 %shard_map.50 = (f32[1024,2304]{1,0:T(8,128)}, bf16[2048,512]{1,0:T(8,128)(2,1)S(1)}, f32[8,8,128]{2,1,0:T(8,128)S(1)}) custom-call(bf16[2048,512]{1,0:T(8,128)(2,1)S(1)} %bitcast.19, f32[8,128]{1,0:T(8,128)S(1)} %pad.7.en_ref), custom_call_target="tpu_custom_call" | custom-call | tf_op jit(solution)/shard_map/pallas_call | solution.py:410
  123.4 0.0 copy-start
  123.4 1.3 copy-done
  124.7 0.6 slice_reduce_fusion
  126.0 0.7 scatter.4.e_ref
  126.7 0.0 copy-start.1
  126.7 81.8 %shard_map.51.x_ref = f32[16,2048]{1,0:T(8,128)} custom-call(f32[1024,2304]{1,0:T(8,128)} %get-tuple-element.17.g_ref, f32[16,2048]{1,0:T(8,128)} %scatter.4.e_ref), custom_call_target="tpu_custom_call" | custom-call | tf_op jit(solution)/shard_map/pallas_call | solution.py:208
  208.5 0.0 slice-start
  208.5 0.0 copy-done.1
  208.5 0.0 copy-start.2
  208.5 0.9 copy-done.2
  209.4 5.5 %shard_map.52 = f32[8,8,512]{2,1,0:T(8,128)S(1)} custom-call(f32[16,2048]{1,0:T(8,128)S(1)} %copy-done.2, bf16[2048,512]{1,0:T(8,128)(2,1)S(1)} %copy-done.1), custom_call_target="tpu_custom_call" | custom-call | tf_op jit(solution)/shard_map/pallas_call | solution.py:453
  215.0 0.6 slice.62
  215.6 0.0 slice-done
  215.6 0.6 constant_dynamic-slice_fusion
  (13 shorter events, 0.2 us)
Async XLA Ops:
  3.7 6.5 %copy-start.3 = (s32[256,100]{0,1:T(8,128)S(1)}, s32[256,100]{0,1:T(8,128)}, u32[]{:S(2)}) copy-start(s32[256,100]{0,1:T(8,128)} %param.6) | copy-start | bytes 307204
  3.8 37.0 %all-to-all-start = ((bf16[256,8,512]{2,0,1:T(8,128)(2,1)}), bf16[256,8,512]{2,0,1:T(8,128)(2,1)S(1)}, u32[]{:S(2)}, u32[]{:S(2)}) async-start(bf16[256,8,512]{2,0,1:T(8,128)(2,1)} %bitcast.20), calls=%async_computation | async-start | bytes 4194304 | tf_op jit(solution)/shard_map/all_to_all | solution.py:486
  10.3 0.7 copy-start.4
  123.4 1.3 copy-start
  126.7 81.8 %copy-start.1 = (bf16[2048,512]{1,0:T(8,128)(2,1)S(1)}, bf16[2048,512]{1,0:T(8,128)(2,1)}, u32[]{:S(2)}) copy-start(bf16[2048,512]{1,0:T(8,128)(2,1)} %copy-done) | copy-start | bytes 6291460
  208.5 7.1 %slice-start = ((f32[16,2048]{1,0:T(8,128)}), f32[1,2048]{1,0:T(1,128)S(1)}, s32[]{:S(2)}) async-start(f32[16,2048]{1,0:T(8,128)} %shard_map.51.x_ref), calls=%async_computation.1 | async-start | bytes 16384 | tf_op jit(solution)/shard_map/slice | solution.py:493
  208.5 1.0 copy-start.2

commit v4 on v3

--- a/solution.py
+++ b/solution.py
@@ -232,6 +232,7 @@
 MESH = pl.DeviceIdType.MESH
 PORTIONS = 6
 STEPS = 6
+CHUNKS = 2
 
 
 def place():
@@ -274,11 +275,14 @@
     return pl.multiple_of(x, 8)
 
 
-def gram_kernel(total, x_ref, en_ref, O, xa, ebuf, F, recv, xp,
-                share_sem, rs_send, rs_recv, ag_send, ag_recv, co_send, co_recv, e_send, e_recv):
+def gram_kernel(total, x_ref, en_ref, O, xa, ebuf, F, recv, raw, xp, relay,
+                share_sem, rs_send, rs_recv, ag_send, ag_recv, co_send, co_recv, e_send, e_recv,
+                a_send, a_recv, own_sem):
     pos, core = place()
     smp, par = lax.axis_index("smp"), lax.axis_index("par")
-    n, kp = x_ref.shape
+    n, kp = raw.shape
+    nr = x_ref.shape[0]
+    kc = kp // CHUNKS
     nb = n // B
     half = F.shape[0]
     width = F.shape[1] // PORTIONS
@@ -290,29 +294,80 @@
     for who in peers:
         pl.semaphore_signal(barrier, inc=1, device_id=who, device_id_type=MESH)
 
+    y, z_lo = lax.div(smp, 2), lax.rem(smp, 2)
+
+    def seat(dy, dz):
+        return lax.rem(y + dy + 4, 4) * 2 + (1 - z_lo if dz else z_lo)
+
+    def sent(to, c):
+        return pl.ds(pl.multiple_of(to * kp + c * kc, kc), kc)
+
+    def landing(origin, row, rows, c):
+        return raw.at[pl.ds(pl.multiple_of(origin * nr + row, rows), rows), c * kc : (c + 1) * kc]
+
+    def straight(c):
+        out = []
+        for i, (dy, dz) in enumerate([(1, 0), (-1, 0), (1, 1), (-1, 1), (0, 1)]):
+            to = seat(dy, dz)
+            out.append(remote(x_ref.at[:, sent(to, c)], landing(smp, 0, nr, c), a_send.at[c, i], a_recv.at[c, i], (to, par)))
+        return out
+
+    def first_leg(c):
+        out = []
+        for d, way in enumerate((1, -1)):
+            for dz in range(2):
+                to = seat(2, dz)
+                out.append(remote(
+                    x_ref.at[d * (nr // 2) : (d + 1) * (nr // 2), sent(to, c)], relay.at[c, d, dz],
+                    a_send.at[c, 5 + 2 * d + dz], a_recv.at[c, 5 + 2 * d + dz], (seat(way, 0), par)))
+        return out
+
+    def second_leg(c):
+        out = []
+        for d, way in enumerate((1, -1)):
+            for dz in range(2):
+                out.append(remote(
+                    relay.at[c, d, dz], landing(seat(-way, 0), d * (nr // 2), nr // 2, c),
+                    a_send.at[c, 9 + 2 * d + dz], a_recv.at[c, 9 + 2 * d + dz], (seat(way, dz), par)))
+        return out
+
+    def begin(c):
+        legs, direct = first_leg(c), straight(c)
+        for copy in legs + direct:
+            copy.start()
+        own = pltpu.make_async_copy(x_ref.at[:, sent(smp, c)], landing(smp, 0, nr, c), own_sem.at[c])
+        own.start()
+        return legs, direct, own
+
+    def pass_on(c, legs):
+        onward = second_leg(c)
+        for leg, copy in zip(legs, onward):
+            leg.wait_recv()
+            copy.start()
+        return onward
+
     scale = 1.0 / np.sqrt(np.float32(total))
 
-    def add(i, acc):
-        r = pl.ds(pl.multiple_of(i * 64, 64), 64)
-        return acc + jnp.sum(x_ref[r, :].astype(jnp.float32).reshape(8, 8, kp), axis=0)
-
-    acc = lax.fori_loop(0, n // 64, add, jnp.zeros((8, kp), jnp.float32))
-    mean = jnp.sum(acc, axis=0, keepdims=True) / total
-
-    @pl.loop(0, n // 64)
-    def _(i):
-        r = pl.ds(pl.multiple_of(i * 64, 64), 64)
-        xa[r, :] = ((x_ref[r, :].astype(jnp.float32) - mean) * scale).astype(jnp.bfloat16)
-
-    ebuf[pl.ds(smp, 1)] = en_ref[...][None]
-    pl.semaphore_wait(barrier, len(peers))
-    share = remote(xa, xp, share_sem.at[0], share_sem.at[1], partner)
-    share.start()
-    spread = [remote(en_ref, ebuf.at[smp], e_send.at[d], e_recv.at[d], others[d]) for d in range(7)]
-    for copy in spread:
-        copy.start()
-
-    def tiles(src, first):
+    def center(c):
+        cols = slice(c * kc, (c + 1) * kc)
+
+        def add(i, acc):
+            r = pl.ds(pl.multiple_of(i * 128, 128), 128)
+            return acc + jnp.sum(raw[r, cols].astype(jnp.float32).reshape(16, 8, kc), axis=0)
+
+        acc = lax.fori_loop(0, n // 128, add, jnp.zeros((8, kc), jnp.float32))
+        mean = jnp.sum(acc, axis=0, keepdims=True) / total
+
+        @pl.loop(0, n // 128)
+        def _(i):
+            r = pl.ds(pl.multiple_of(i * 128, 128), 128)
+            xa[r, cols] = ((raw[r, cols].astype(jnp.float32) - mean) * scale).astype(jnp.bfloat16)
+
+        share = remote(xa.at[:, cols], xp.at[:, cols], share_sem.at[c, 0], share_sem.at[c, 1], partner)
+        share.start()
+        return share
+
+    def tiles(src, c, first):
         @pl.loop(0, 2 * (nb + 1))
         def _(t):
             a_local = lax.div(t, nb + 1)
@@ -321,15 +376,36 @@
             tall = j < nb - a
             r = jnp.where(tall, nb - 1 - a, a)
             cb = jnp.where(tall, j, j - (nb - a))
-            rows = src[pl.ds(pl.multiple_of(r * B, B), B), :]
-            cols = src[pl.ds(pl.multiple_of(cb * B, B), B), :]
+            rows = src[pl.ds(pl.multiple_of(r * B, B), B), c * kc : (c + 1) * kc]
+            cols = src[pl.ds(pl.multiple_of(cb * B, B), B), c * kc : (c + 1) * kc]
             got = lax.dot_general(rows, cols, (NT, ((), ())), preferred_element_type=jnp.float32)
             at = (pl.ds(pl.multiple_of(a_local * B, B), B), pl.ds(pl.multiple_of(j * B, B), B))
             F[at] = got if first else F[at] + got
 
-    tiles(xa, True)
-    share.wait_recv()
-    tiles(xp, False)
+    ebuf[pl.ds(smp, 1)] = en_ref[...][None]
+    pl.semaphore_wait(barrier, len(peers))
+    shares, moved = [], []
+    flight = begin(0)
+    for c in range(CHUNKS):
+        legs, direct, own = flight
+        onward = pass_on(c, legs)
+        if c + 1 < CHUNKS:
+            flight = begin(c + 1)
+        else:
+            spread = [remote(en_ref, ebuf.at[smp], e_send.at[d], e_recv.at[d], others[d]) for d in range(7)]
+            for copy in spread:
+                copy.start()
+        for copy in direct + onward:
+            copy.wait_recv()
+        own.wait()
+        moved += legs + direct + onward
+        shares.append(center(c))
+        tiles(xa, c, c == 0)
+        if c > 0:
+            shares[c - 1].wait_recv()
+            tiles(xp, c - 1, False)
+    shares[-1].wait_recv()
+    tiles(xp, CHUNKS - 1, False)
 
     def cols(q):
         return slice(q * width, q * width + width)
@@ -391,7 +467,8 @@
                 back[t - 1, q].start()
             forth.append(across(t, q, base[q][t] + (1 - plans[q][t][1]) * size[t], size[t]))
             forth[-1].start()
-    share.wait_send()
+    for copy in shares + moved:
+        copy.wait_send()
     for copy in spread:
         copy.wait()
     for copy in [*copies.values(), *back.values()]:
@@ -400,8 +477,9 @@
         copy.wait()
 
 
-def damped_gram(mine, energy, total):
-    n, kp = mine.shape
+def damped_gram(log_derivs, energy, total):
+    n, kp = total, log_derivs.shape[1] // 8
+    nr = log_derivs.shape[0]
     nb = n // B
     wide = (nb + 1) * B
     vm = pl.BlockSpec(memory_space=pltpu.VMEM)
@@ -414,19 +492,22 @@
             jax.ShapeDtypeStruct((n, kp), jnp.bfloat16),
             jax.ShapeDtypeStruct((8, 8, 128), jnp.float32),
         ],
-        in_specs=[vm, vm],
+        in_specs=[pl.BlockSpec(memory_space=pl.ANY), vm],
         out_specs=[vm, vm, vm],
         scratch_shapes=[
             pltpu.VMEM((n // 4, wide), jnp.float32),
             pltpu.VMEM((n // 4, wide), jnp.float32),
             pltpu.VMEM((n, kp), jnp.bfloat16),
-            dma((2,)), dma(grid), dma(grid), dma(grid), dma(grid),
+            pltpu.VMEM((n, kp), jnp.bfloat16),
+            pltpu.VMEM((CHUNKS, 2, 2, nr // 2, kp // CHUNKS), jnp.bfloat16),
+            dma((CHUNKS, 2)), dma(grid), dma(grid), dma(grid), dma(grid),
             dma((STEPS + 1, PORTIONS)), dma((STEPS + 1, PORTIONS)), dma((7,)), dma((7,)),
+            dma((CHUNKS, 13)), dma((CHUNKS, 13)), dma((CHUNKS,)),
         ],
         compiler_params=pltpu.CompilerParams(
             vmem_limit_bytes=48 * 2**20, collective_id=1, has_side_effects=True
         ),
-    )(mine, energy)
+    )(log_derivs, energy)
 
 
 def update_kernel(x_ref, xc_ref, u_ref, send, recv):
@@ -483,8 +564,7 @@
     scale = 1.0 / jnp.sqrt(jnp.float32(total))
     energy = local_energy(spins) + hop_energy
     energy = jnp.pad(energy.reshape(rows // 128, 128), ((0, 8 - rows // 128), (0, 0)))
-    mine = lax.all_to_all(log_derivs, "smp", split_axis=1, concat_axis=0, tiled=True)
-    gram, centered, energies = damped_gram(mine, energy, total)
+    gram, centered, energies = damped_gram(log_derivs, energy, total)
     all_energy = energies[:, : rows // 128].reshape(-1)
     eps = (all_energy - jnp.mean(all_energy)) * scale
     coeffs = solve(gram, eps)

time: 216 us -> 210 us (0.972)
  Pallas kernels: 170 us -> 203 us
  waiting for transfers between devices: 29.8 us -> 0 us
  starting transfers between devices: 6.51 us -> 0 us
  local copies, waits for them, and re-layouts: 7.61 us -> 4.41 us
    pallas_call x1, Pallas kernels: 82.7 us -> 115 us  [damped_gram(): pl.pallas_call(functools.partial(gram_kernel, total), out_shape=[jax.Shap...]
    all_to_all x1 -> x0, waiting for transfers between devices: 29.8 us -> none  [body(): lax.all_to_all(log_derivs, 'smp', split_axis=1, concat_axis=0, tiled=True)]
    all_to_all x1 -> x0, starting transfers between devices: 6.51 us -> none  [body(): lax.all_to_all(log_derivs, 'smp', split_axis=1, concat_axis=0, tiled=True)]
    all_to_all x1 -> x0, local copies, waits for them, and re-layouts: 3.12 us -> none  [body(): lax.all_to_all(log_derivs, 'smp', split_axis=1, concat_axis=0, tiled=True)]
  transfers between devices with their start and end apart: 1 -> 0, of which waited for: 1 -> 0; matrix products, arithmetic and copies ran while one was open for 0% -> 0% of each run, Pallas kernels for 0% -> 0%
where the time goes in v4:
time: 210 us
  Pallas kernels  203 us (97%)
  local copies, waits for them, and re-layouts  4.41 us (2%)
    pallas_call x1, Pallas kernels, damped_gram(): pl.pallas_call(functools.partial(gram_kernel, total), out_shape=[jax.Shap...  115 us
    pallas_call x1, Pallas kernels, solve(): pl.pallas_call(functools.partial(kernel, n), out_shape=jax.ShapeDtypeStru...  81.6 us
    pallas_call x1, Pallas kernels, project(): pl.pallas_call(update_kernel, out_shape=jax.ShapeDtypeStruct((8, 8, xc.sh...  6.13 us

profile of v4, /device:TPU:1, one launch (start us, length us, event | category | flops | bytes accessed | tf_op | source)
XLA Modules:
  0.0 210.2 jit_solution(13830484664381202691)
XLA Ops:
  0.6 0.0 copy-start.2
  0.6 0.0 copy-start.3
  0.6 1.0 add_convert_fusion
  1.7 0.1 maximum_add_fusion
  1.9 0.0 copy-done.2
  1.9 0.1 multiply_reduce_fusion.1
  2.0 0.0 copy-done.3
  2.0 0.0 copy-start
  2.0 1.6 copy-done
  3.6 114.8 %shard_map.50 = (f32[1024,2304]{1,0:T(8,128)}, bf16[2048,512]{1,0:T(8,128)(2,1)S(1)}, f32[8,8,128]{2,1,0:T(8,128)S(1)}) custom-call(bf16[256,4096]{1,0:T(8,128)(2,1)S(1)} %copy-done, f32[8,128]{1,0:T(8,128)S(1)} %pad.7.en_ref), custom_call_target="tpu_custom_call" | custom-call | tf_op jit(solution)/shard_map/pallas_call | solution.py:488
  118.4 0.6 slice_reduce_fusion
  119.7 0.7 scatter.4.e_ref
  120.3 81.6 %shard_map.51.x_ref = f32[16,2048]{1,0:T(8,128)} custom-call(f32[1024,2304]{1,0:T(8,128)} %get-tuple-element.17.g_ref, f32[16,2048]{1,0:T(8,128)} %scatter.4.e_ref), custom_call_target="tpu_custom_call" | custom-call | tf_op jit(solution)/shard_map/pallas_call | solution.py:208
  202.0 0.0 copy-start.1
  202.0 0.9 copy-done.1
  202.9 0.0 slice-start
  202.9 6.1 %shard_map.52 = f32[8,8,512]{2,1,0:T(8,128)S(1)} custom-call(f32[16,2048]{1,0:T(8,128)S(1)} %copy-done.1, bf16[2048,512]{1,0:T(8,128)(2,1)S(1)} %get-tuple-element.19.xc_ref), custom_call_target="tpu_custom_call" | custom-call | tf_op jit(solution)/shard_map/pallas_call | solution.py:534
  209.0 0.6 slice.62
  209.6 0.0 slice-done
  209.6 0.6 constant_dynamic-slice_fusion
  (12 shorter events, 0.2 us)
Async XLA Ops:
  0.6 1.3 copy-start.2
  0.6 1.3 copy-start.3
  2.0 1.6 copy-start
  202.0 0.9 copy-start.1
  202.9 6.8 %slice-start = ((f32[16,2048]{1,0:T(8,128)}), f32[1,2048]{1,0:T(1,128)S(1)}, s32[]{:S(2)}) async-start(f32[16,2048]{1,0:T(8,128)} %shard_map.51.x_ref), calls=%async_computation | async-start | bytes 16384 | tf_op jit(solution)/shard_map/slice | solution.py:573

commit v5 on v4

--- a/solution.py
+++ b/solution.py
@@ -93,11 +93,31 @@
     return [jnp.where(lane <= sub + 8 * g, out[g], 0.0) for g in range(16)]
 
 
+def slot(nb, i, k):
+    return nb * k - lax.div(k * (k - 1), 2) + i - k
+
+
 def tile(nb, i, k):
-    upper = i >= nb // 2
-    a = jnp.where(upper, nb - 1 - i, i)
-    j = jnp.where(upper, k, nb - i + k)
-    return pl.ds(pl.multiple_of(a * B, B), B), pl.ds(pl.multiple_of(j * B, B), B)
+    t = slot(nb, i, k)
+    a, j = lax.rem(t, PACK), lax.div(t, PACK)
+    return lax.div(j, 3), 2 * lax.rem(j, 3), pl.multiple_of(a * B, B)
+
+
+def get(G, at):
+    s, q, r = at
+    return jnp.concatenate([G[s, q, pl.ds(r, B), :], G[s, q + 1, pl.ds(r, B), :]], axis=1)
+
+
+def put(G, at, value):
+    s, q, r = at
+    G[s, q, pl.ds(r, B), :] = value[:, 0:H]
+    G[s, q + 1, pl.ds(r, B), :] = value[:, H:B]
+
+
+def sub(G, at, value):
+    s, q, r = at
+    G[s, q, pl.ds(r, B), :] -= value[:, 0:H]
+    G[s, q + 1, pl.ds(r, B), :] -= value[:, H:B]
 
 
 def block(i):
@@ -105,11 +125,12 @@
 
 
 SLOTS = 8
+PACK = 4
 
 
 def kernel(n, g_ref, e_ref, x_ref, G, lhi, llo, ec, whi, wlo, D, W, T, R, A2, z, sem):
     nb = n // B
-    load = pltpu.make_async_copy(g_ref, G.at[0 : n // 2, :], sem)
+    load = pltpu.make_async_copy(g_ref, G.at[:, :, 0 : n // 2, :], sem)
     load.start()
     ec[...] = e_ref[...]
     diag = lax.broadcasted_iota(jnp.int32, (H, H), 0) == lax.broadcasted_iota(jnp.int32, (H, H), 1)
@@ -117,7 +138,7 @@
     load.wait()
 
     def triangle(k, i):
-        ch, cl = split(G[tile(nb, i, k)])
+        ch, cl = split(get(G, tile(nb, i, k)))
         th, tl = split(dot3(ch, cl, whi[k], wlo[k], NT))
         lhi[block(i), block(k)], llo[block(i), block(k)] = th, tl
         yh, yl = split(z[:, block(k)])
@@ -135,11 +156,11 @@
             own = u == k
             column = jnp.where(own, k, jnp.minimum(k + 1, nb - 1))
             j = jnp.where(own, k - 1, u)
-            rows, cols = tile(nb, i, column)
-            rows = pl.ds(pl.multiple_of(jnp.where(live, rows.start, n // 2), B), B)
-            G[rows, cols] -= dot3(
+            at = tile(nb, i, column)
+            at = (at[0], at[1], pl.multiple_of(jnp.where(live, at[2], n // 2), B))
+            sub(G, at, dot3(
                 lhi[block(i), block(j)], llo[block(i), block(j)],
-                lhi[block(column), block(j)], llo[block(column), block(j)], NT)
+                lhi[block(column), block(j)], llo[block(column), block(j)], NT))
 
         got = factor_inverse([D[8 * g : 8 * g + 8, :] for g in range(16)], T, R, A2, beside if slots else None)
         for g in range(16):
@@ -157,26 +178,25 @@
             factor(k, h, False)
 
     def panel(k, _):
-        rows, cols = tile(nb, k, k)
-        r0, c0 = rows.start, cols.start
+        home = tile(nb, k, k)
 
         @pl.when(k > 0)
         def _():
             th, tl = triangle(k - 1, k)
-            G[rows, cols] -= dot3(th, tl, th, tl, NT)
+            sub(G, home, dot3(th, tl, th, tl, NT))
 
             @pl.loop(k + 1, nb)
             def _(i):
                 triangle(k - 1, i)
 
-        top, low = pl.ds(r0, H), pl.ds(pl.multiple_of(r0 + H, H), H)
-        left, right = pl.ds(c0, H), pl.ds(pl.multiple_of(c0 + H, H), H)
-        D[...] = G[top, left] + damp
+        hs, hq, hr = home
+        top, low = pl.ds(hr, H), pl.ds(pl.multiple_of(hr + H, H), H)
+        D[...] = G[hs, hq, top, :] + damp
         chain(k, 0)
         w1h, w1l = split(W[0])
-        ah, al = split(G[low, left])
+        ah, al = split(G[hs, hq, low, :])
         lh, ll = split(dot3(ah, al, w1h, w1l, NT))
-        D[...] = G[low, right] + damp - dot3(lh, ll, lh, ll, NT)
+        D[...] = G[hs, hq + 1, low, :] + damp - dot3(lh, ll, lh, ll, NT)
         th, tl = split(dot3(lh, ll, w1h, w1l, NN))
         whi[k, 0:H, 0:H], wlo[k, 0:H, 0:H] = w1h, w1l
         whi[k, 0:H, H:B] = jnp.zeros((H, H), jnp.bfloat16)
@@ -211,7 +231,7 @@
         in_specs=[pl.BlockSpec(memory_space=pl.ANY), vm],
         out_specs=vm,
         scratch_shapes=[
-            pltpu.VMEM((n // 2 + B, (nb + 1) * B), jnp.float32),
+            pltpu.VMEM((3, 6, n // 2 + B, H), jnp.float32),
             pltpu.VMEM((n, n), jnp.bfloat16),
             pltpu.VMEM((n, n), jnp.bfloat16),
             pltpu.VMEM((16, n), jnp.float32),
@@ -231,7 +251,6 @@
 
 MESH = pl.DeviceIdType.MESH
 PORTIONS = 6
-STEPS = 6
 CHUNKS = 2
 
 
@@ -248,21 +267,25 @@
 
 
 def plan(pos, core, q):
-    out = []
-    for stage in range(3):
-        axis = (q // 2 + stage) % 3
-        i = pos[axis]
-        low, high = lax.rem(i, 2), lax.div(i, 2)
-        near, far = i + 1 - 2 * low, 3 - i
-        if q % 2 == 0:
-            order = [(near, lax.rem(low + high, 2)), (far, high)]
-        else:
-            order = [(far, high), (near, low)]
-        for other, bit in order:
-            there = list(pos)
-            there[axis] = other
-            out.append((device(there, core), bit))
-    return out
+    first = q // 2
+
+    def at(axis, i):
+        there = list(pos)
+        there[axis] = i
+        return device(there, core)
+
+    i = pos[first]
+    low, high = lax.rem(i, 2), lax.div(i, 2)
+    near, far = at(first, i + 1 - 2 * low), at(first, 3 - i)
+    if q % 2 == 0:
+        halves = [(near, lax.rem(low + high, 2)), (far, high)]
+    else:
+        halves = [(far, high), (near, low)]
+    cuts = []
+    for stage in (1, 2):
+        axis = (first + stage) % 3
+        cuts.append((pos[axis], [at(axis, lax.rem(pos[axis] + d, 4)) for d in (1, 2, 3)]))
+    return halves, cuts
 
 
 def remote(src, dst, send, recv, who):
@@ -276,7 +299,7 @@
 
 
 def gram_kernel(total, x_ref, en_ref, O, xa, ebuf, F, recv, raw, xp, relay,
-                share_sem, rs_send, rs_recv, ag_send, ag_recv, co_send, co_recv, e_send, e_recv,
+                share_sem, c_send, c_recv, e_send, e_recv,
                 a_send, a_recv, own_sem):
     pos, core = place()
     smp, par = lax.axis_index("smp"), lax.axis_index("par")
@@ -284,12 +307,11 @@
     nr = x_ref.shape[0]
     kc = kp // CHUNKS
     nb = n // B
-    half = F.shape[0]
-    width = F.shape[1] // PORTIONS
+    half = F.shape[2]
     plans = [plan(pos, core, q) for q in range(PORTIONS)]
     partner = device(pos, 1 - core)
     others = [(lax.rem(smp + d, 8), par) for d in range(1, 8)]
-    peers = [partner] + [plans[2 * a][s][0] for a in range(3) for s in range(2)] + others
+    peers = [partner] + [who for q in (0, 2, 4) for who in plans[q][1][0][1]] + others
     barrier = pltpu.get_barrier_semaphore()
     for who in peers:
         pl.semaphore_signal(barrier, inc=1, device_id=who, device_id_type=MESH)
@@ -367,24 +389,25 @@
         share.start()
         return share
 
+    starts = [nb * k - k * (k - 1) // 2 for k in range(1, nb)]
+
     def tiles(src, c, first):
         @pl.loop(0, 2 * (nb + 1))
-        def _(t):
-            a_local = lax.div(t, nb + 1)
-            j = lax.rem(t, nb + 1)
-            a = core * (nb // 4) + a_local
-            tall = j < nb - a
-            r = jnp.where(tall, nb - 1 - a, a)
-            cb = jnp.where(tall, j, j - (nb - a))
-            rows = src[pl.ds(pl.multiple_of(r * B, B), B), c * kc : (c + 1) * kc]
-            cols = src[pl.ds(pl.multiple_of(cb * B, B), B), c * kc : (c + 1) * kc]
+        def _(it):
+            a_local, j = lax.rem(it, 2), lax.div(it, 2)
+            t = PACK * j + 2 * core + a_local
+            k = sum(jnp.where(t >= start, 1, 0) for start in starts)
+            i = t - (nb * k - lax.div(k * (k - 1), 2)) + k
+            rows = src[block(i), c * kc : (c + 1) * kc]
+            cols = src[block(k), c * kc : (c + 1) * kc]
             got = lax.dot_general(rows, cols, (NT, ((), ())), preferred_element_type=jnp.float32)
-            at = (pl.ds(pl.multiple_of(a_local * B, B), B), pl.ds(pl.multiple_of(j * B, B), B))
-            F[at] = got if first else F[at] + got
+            at = (lax.div(j, 3), 2 * lax.rem(j, 3), pl.multiple_of(a_local * B, B))
+            put(F, at, got if first else get(F, at) + got)
 
     ebuf[pl.ds(smp, 1)] = en_ref[...][None]
     pl.semaphore_wait(barrier, len(peers))
     shares, moved = [], []
+    spread = [remote(en_ref, ebuf.at[smp], e_send.at[d], e_recv.at[d], others[d]) for d in range(7)]
     flight = begin(0)
     for c in range(CHUNKS):
         legs, direct, own = flight
@@ -392,7 +415,6 @@
         if c + 1 < CHUNKS:
             flight = begin(c + 1)
         else:
-            spread = [remote(en_ref, ebuf.at[smp], e_send.at[d], e_recv.at[d], others[d]) for d in range(7)]
             for copy in spread:
                 copy.start()
         for copy in direct + onward:
@@ -401,107 +423,142 @@
         moved += legs + direct + onward
         shares.append(center(c))
         tiles(xa, c, c == 0)
-        if c > 0:
-            shares[c - 1].wait_recv()
-            tiles(xp, c - 1, False)
-    shares[-1].wait_recv()
-    tiles(xp, CHUNKS - 1, False)
-
-    def cols(q):
-        return slice(q * width, q * width + width)
-
-    offs = [half - (half >> t) for t in range(STEPS)]
-    size = [half >> (t + 1) for t in range(STEPS)]
-    base = [[jnp.int32(0)] for q in range(PORTIONS)]
-
-    def halving(t, q):
-        who, bit = plans[q][t]
-        src = F.at[pl.ds(eight(base[q][t] + (1 - bit) * size[t]), size[t]), cols(q)]
-        return remote(src, recv.at[pl.ds(offs[t], size[t]), cols(q)], rs_send.at[t, q], rs_recv.at[t, q], who)
-
-    def accumulate(t, q, start, rows):
-        at = (pl.ds(eight(base[q][t + 1] + start), rows), cols(q))
-        F[at] += recv[pl.ds(eight(offs[t] + start), rows), cols(q)]
-
-    copies = {}
-    for q in range(PORTIONS):
-        copies[0, q] = halving(0, q)
-        copies[0, q].start()
-    for t in range(STEPS):
-        for q in range(PORTIONS):
-            copies[t, q].wait_recv()
-            base[q].append(base[q][t] + plans[q][t][1] * size[t])
-            if t + 1 < STEPS:
-                bit, s = plans[q][t + 1][1], size[t + 1]
-                accumulate(t, q, (1 - bit) * s, s)
-                copies[t + 1, q] = halving(t + 1, q)
-                copies[t + 1, q].start()
-                accumulate(t, q, bit * s, s)
-            else:
-                accumulate(t, q, 0, size[t])
-
-    def region(row, rows, q):
-        return O.at[pl.ds(eight(core * half + row), rows), cols(q)]
-
-    def doubling(t, q):
-        here = region(base[q][t + 1], size[t], q)
-        return remote(here, here, ag_send.at[t, q], ag_recv.at[t, q], plans[q][t][0])
-
-    def across(t, q, row, rows):
-        here = region(row, rows, q)
-        return remote(here, here, co_send.at[t, q], co_recv.at[t, q], partner)
-
-    back, forth = {}, []
-    for q in range(PORTIONS):
-        row, rows = base[q][STEPS], size[STEPS - 1]
-        O[pl.ds(eight(core * half + row), rows), cols(q)] = F[pl.ds(eight(row), rows), cols(q)]
-        back[STEPS - 1, q] = doubling(STEPS - 1, q)
-        back[STEPS - 1, q].start()
-        forth.append(across(STEPS, q, row, rows))
-        forth[-1].start()
-    for t in range(STEPS - 1, -1, -1):
-        for q in range(PORTIONS):
-            back[t, q].wait_recv()
-            if t > 0:
-                back[t - 1, q] = doubling(t - 1, q)
-                back[t - 1, q].start()
-            forth.append(across(t, q, base[q][t] + (1 - plans[q][t][1]) * size[t], size[t]))
-            forth[-1].start()
-    for copy in shares + moved:
+        shares[c].wait_recv()
+        tiles(xp, c, False)
+    portions = range(PORTIONS)
+    base = []
+    for q in portions:
+        rows, at = half, jnp.int32(0)
+        base.append([at])
+        for _, bit in plans[q][0]:
+            rows = rows // 2
+            at = at + bit * rows
+            base[q].append(at)
+        for i, _ in plans[q][1]:
+            rows = rows // 4
+            at = at + i * rows
+            base[q].append(at)
+    size = [half, half // 2, half // 4, half // 16, half // 64]
+    offs = [0, size[1], size[1] + size[2], size[1] + size[2] + 3 * size[3]]
+
+    def part(ref, q, row, rows):
+        return ref.at[:, q, pl.ds(eight(row), rows), :]
+
+    def accumulate(q, row, rows, held):
+        at = (slice(None), q, pl.ds(eight(row), rows), slice(None))
+        F[at] += recv[:, q, pl.ds(eight(held), rows), :]
+
+    sem = iter(range(10**6))
+    pending = []
+
+    def go(src, dst, who):
+        i = next(sem)
+        copy = remote(src, dst, c_send.at[i], c_recv.at[i], who)
+        copy.start()
+        pending.append(copy)
+        return copy
+
+    def halve(q, t):
+        who, bit = plans[q][0][t]
+        row = base[q][t] + (1 - bit) * size[t + 1]
+        return go(part(F, q, row, size[t + 1]), part(recv, q, offs[t], size[t + 1]), who)
+
+    def cut(q, stage):
+        i, whos = plans[q][1][stage]
+        rows = size[stage + 3]
+        out = []
+        for d, who in enumerate(whos):
+            row = base[q][stage + 2] + lax.rem(i + d + 1, 4) * rows
+            out.append(go(part(F, q, row, rows), part(recv, q, offs[stage + 2] + d * rows, rows), who))
+        return out
+
+    one = [halve(q, 0) for q in portions]
+    two, three, four = [], [], []
+    for q in portions:
+        one[q].wait_recv()
+        bit, rows = plans[q][0][1][1], size[2]
+        accumulate(q, base[q][1] + (1 - bit) * rows, rows, offs[0] + (1 - bit) * rows)
+        two.append(halve(q, 1))
+        accumulate(q, base[q][2], rows, offs[0] + bit * rows)
+    for q in portions:
+        two[q].wait_recv()
+        accumulate(q, base[q][2], size[2], offs[1])
+        three.append(cut(q, 0))
+    for q in portions:
+        for d, copy in enumerate(three[q]):
+            copy.wait_recv()
+            accumulate(q, base[q][3], size[3], offs[2] + d * size[3])
+        four.append(cut(q, 1))
+    for q in portions:
+        for d, copy in enumerate(four[q]):
+            copy.wait_recv()
+            accumulate(q, base[q][4], size[4], offs[3] + d * size[4])
+        at = pl.ds(eight(core * half + base[q][4]), size[4])
+        O[:, q, at, :] = F[:, q, pl.ds(eight(base[q][4]), size[4]), :]
+    def region(q, row, rows):
+        return part(O, q, core * half + row, rows)
+
+    def spread_out(q, stage):
+        here = region(q, base[q][stage + 3], size[stage + 3])
+        return [go(here, here, who) for who in plans[q][1][stage][1]]
+
+    def double(q, t):
+        here = region(q, base[q][t + 1], size[t + 1])
+        return go(here, here, plans[q][0][t][0])
+
+    def across(q, row):
+        here = region(q, row, size[1])
+        return go(here, here, partner)
+
+    five, six, seven, eighth, over = [], [], [], [], []
+    for q in portions:
+        five.append(spread_out(q, 1))
+    for q in portions:
+        for copy in five[q]:
+            copy.wait_recv()
+        six.append(spread_out(q, 0))
+    for q in portions:
+        for copy in six[q]:
+            copy.wait_recv()
+        seven.append(double(q, 1))
+    for q in portions:
+        seven[q].wait_recv()
+        eighth.append(double(q, 0))
+        over.append(across(q, base[q][1]))
+    for q in portions:
+        eighth[q].wait_recv()
+        over.append(across(q, size[1] - base[q][1]))
+    for copy in over:
+        copy.wait_recv()
+    for copy in pending:
         copy.wait_send()
     for copy in spread:
         copy.wait()
-    for copy in [*copies.values(), *back.values()]:
+    for copy in shares + moved:
         copy.wait_send()
-    for copy in forth:
-        copy.wait()
 
 
 def damped_gram(log_derivs, energy, total):
     n, kp = total, log_derivs.shape[1] // 8
     nr = log_derivs.shape[0]
-    nb = n // B
-    wide = (nb + 1) * B
     vm = pl.BlockSpec(memory_space=pltpu.VMEM)
     dma = pltpu.SemaphoreType.DMA
-    grid = (STEPS, PORTIONS)
     return pl.pallas_call(
         functools.partial(gram_kernel, total),
         out_shape=[
-            jax.ShapeDtypeStruct((n // 2, wide), jnp.float32),
+            jax.ShapeDtypeStruct((3, PORTIONS, n // 2, H), jnp.float32),
             jax.ShapeDtypeStruct((n, kp), jnp.bfloat16),
             jax.ShapeDtypeStruct((8, 8, 128), jnp.float32),
         ],
         in_specs=[pl.BlockSpec(memory_space=pl.ANY), vm],
         out_specs=[vm, vm, vm],
         scratch_shapes=[
-            pltpu.VMEM((n // 4, wide), jnp.float32),
-            pltpu.VMEM((n // 4, wide), jnp.float32),
+            pltpu.VMEM((3, PORTIONS, n // 4, H), jnp.float32),
+            pltpu.VMEM((3, PORTIONS, n // 4, H), jnp.float32),
             pltpu.VMEM((n, kp), jnp.bfloat16),
             pltpu.VMEM((n, kp), jnp.bfloat16),
             pltpu.VMEM((CHUNKS, 2, 2, nr // 2, kp // CHUNKS), jnp.bfloat16),
-            dma((CHUNKS, 2)), dma(grid), dma(grid), dma(grid), dma(grid),
-            dma((STEPS + 1, PORTIONS)), dma((STEPS + 1, PORTIONS)), dma((7,)), dma((7,)),
+            dma((CHUNKS, 2)), dma((18 * PORTIONS,)), dma((18 * PORTIONS,)), dma((7,)), dma((7,)),
             dma((CHUNKS, 13)), dma((CHUNKS, 13)), dma((CHUNKS,)),
         ],
         compiler_params=pltpu.CompilerParams(

time: 210 us -> 201 us (0.957)
  Pallas kernels: 203 us -> 193 us
    pallas_call x1, Pallas kernels: 115 us -> 106 us  [damped_gram(): pl.pallas_call(functools.partial(gram_kernel, total), out_shape=[jax.Shap...]
where the time goes in v5:
time: 201 us; the launch traced here: 200 us
  Pallas kernels  193 us (96%)
  local copies, waits for them, and re-layouts  4.41 us (2%)
    pallas_call x1, Pallas kernels, damped_gram(): pl.pallas_call(functools.partial(gram_kernel, total), out_shape=[jax.Shap...  106 us
    pallas_call x1, Pallas kernels, solve(): pl.pallas_call(functools.partial(kernel, n), out_shape=jax.ShapeDtypeStru...  81.1 us
    pallas_call x1, Pallas kernels, project(): pl.pallas_call(update_kernel, out_shape=jax.ShapeDtypeStruct((8, 8, xc.sh...  5.67 us

profile of v5, /device:TPU:1, one launch (start us, length us, event | category | flops | bytes accessed | tf_op | source)
XLA Modules:
  0.0 200.4 jit_solution(11815942929343029661)
XLA Ops:
  0.6 0.0 copy-start.2
  0.6 0.0 copy-start.3
  0.6 1.0 add_convert_fusion
  1.7 0.1 maximum_add_fusion
  1.9 0.0 copy-done.2
  1.9 0.1 multiply_reduce_fusion.1
  2.0 0.0 copy-done.3
  2.0 0.0 copy-start
  2.0 1.6 copy-done
  3.6 106.0 %shard_map.50 = (f32[3,6,1024,128]{3,2,1,0:T(8,128)}, bf16[2048,512]{1,0:T(8,128)(2,1)S(1)}, f32[8,8,128]{2,1,0:T(8,128)S(1)}) custom-call(bf16[256,4096]{1,0:T(8,128)(2,1)S(1)} %copy-done, f32[8,128]{1,0:T(8,128)S(1)} %pad.7.en_ref), custom_call_target="tpu_custom_call" | custom-call | tf_op jit(solution)/shard_map/pallas_call | solution.py:546
  109.5 0.6 slice_reduce_fusion
  110.8 0.7 scatter.4.e_ref
  111.5 81.1 %shard_map.51.x_ref = f32[16,2048]{1,0:T(8,128)} custom-call(f32[3,6,1024,128]{3,2,1,0:T(8,128)} %get-tuple-element.17.g_ref, f32[16,2048]{1,0:T(8,128)} %scatter.4.e_ref), custom_call_target="tpu_custom_call" | custom-call | tf_op jit(solution)/shard_map/pallas_call | solution.py:228
  192.6 0.0 copy-start.1
  192.6 0.9 copy-done.1
  193.5 0.0 slice-start
  193.5 5.7 %shard_map.52 = f32[8,8,512]{2,1,0:T(8,128)S(1)} custom-call(f32[16,2048]{1,0:T(8,128)S(1)} %copy-done.1, bf16[2048,512]{1,0:T(8,128)(2,1)S(1)} %get-tuple-element.19.xc_ref), custom_call_target="tpu_custom_call" | custom-call | tf_op jit(solution)/shard_map/pallas_call | solution.py:591
  199.2 0.6 slice.62
  199.8 0.0 slice-done
  199.8 0.6 constant_dynamic-slice_fusion
  (12 shorter events, 0.2 us)
Async XLA Ops:
  0.6 1.3 copy-start.2
  0.6 1.3 copy-start.3
  2.0 1.6 copy-start
  192.6 0.9 copy-start.1
  193.5 6.3 %slice-start = ((f32[16,2048]{1,0:T(8,128)}), f32[1,2048]{1,0:T(1,128)S(1)}, s32[]{:S(2)}) async-start(f32[16,2048]{1,0:T(8,128)} %shard_map.51.x_ref), calls=%async_computation | async-start | bytes 16384 | tf_op jit(solution)/shard_map/slice | solution.py:630

commit v6 on v5

--- a/solution.py
+++ b/solution.py
@@ -128,20 +128,19 @@
 PACK = 4
 
 
-def kernel(n, g_ref, e_ref, x_ref, G, lhi, llo, ec, whi, wlo, D, W, T, R, A2, z, sem):
+def solve(n, x_ref, G, lhi, llo, ec, whi, wlo, D, W, T, R, A2, z, hooks):
     nb = n // B
-    load = pltpu.make_async_copy(g_ref, G.at[:, :, 0 : n // 2, :], sem)
-    load.start()
-    ec[...] = e_ref[...]
     diag = lax.broadcasted_iota(jnp.int32, (H, H), 0) == lax.broadcasted_iota(jnp.int32, (H, H), 1)
     damp = jnp.where(diag, jnp.float32(0.2), jnp.float32(0.0))
-    load.wait()
+
+    def span(k):
+        return slice(k * B, k * B + B) if isinstance(k, int) else block(k)
 
     def triangle(k, i):
         ch, cl = split(get(G, tile(nb, i, k)))
         th, tl = split(dot3(ch, cl, whi[k], wlo[k], NT))
-        lhi[block(i), block(k)], llo[block(i), block(k)] = th, tl
-        yh, yl = split(z[:, block(k)])
+        lhi[block(i), span(k)], llo[block(i), span(k)] = th, tl
+        yh, yl = split(z[:, span(k)])
         ec[:, block(i)] -= dot3(yh, yl, th, tl, NT)
         return th, tl
 
@@ -167,21 +166,22 @@
             W[h, 8 * g : 8 * g + 8, :] = got[g]
 
     def chain(k, h):
-        some = (k > 0) & (k < nb - 1)
-
-        @pl.when(some)
+        if isinstance(k, int):
+            factor(k, h, False)
+            return
+
+        @pl.when(k < nb - 1)
         def _():
             factor(k, h, True)
 
-        @pl.when(jnp.logical_not(some))
+        @pl.when(k == nb - 1)
         def _():
             factor(k, h, False)
 
-    def panel(k, _):
-        home = tile(nb, k, k)
-
-        @pl.when(k > 0)
-        def _():
+    def panel(k):
+        first = isinstance(k, int)
+        home = (0, 0, 0) if first else tile(nb, k, k)
+        if not first:
             th, tl = triangle(k - 1, k)
             sub(G, home, dot3(th, tl, th, tl, NT))
 
@@ -190,9 +190,13 @@
                 triangle(k - 1, i)
 
         hs, hq, hr = home
-        top, low = pl.ds(hr, H), pl.ds(pl.multiple_of(hr + H, H), H)
+        top, low = (pl.ds(0, H), pl.ds(H, H)) if first else (pl.ds(hr, H), pl.ds(pl.multiple_of(hr + H, H), H))
         D[...] = G[hs, hq, top, :] + damp
+        if first:
+            hooks[0]()
         chain(k, 0)
+        if first:
+            hooks[1]()
         w1h, w1l = split(W[0])
         ah, al = split(G[hs, hq, low, :])
         lh, ll = split(dot3(ah, al, w1h, w1l, NT))
@@ -202,14 +206,24 @@
         whi[k, 0:H, H:B] = jnp.zeros((H, H), jnp.bfloat16)
         wlo[k, 0:H, H:B] = jnp.zeros((H, H), jnp.bfloat16)
         chain(k, 1)
+        if first:
+            hooks[2]()
         w2h, w2l = split(W[1])
         whi[k, H:B, H:B], wlo[k, H:B, H:B] = w2h, w2l
         whi[k, H:B, 0:H], wlo[k, H:B, 0:H] = split(-dot3(w2h, w2l, th, tl, NN))
-        eh, el = split(ec[:, block(k)])
-        z[:, block(k)] = dot3(eh, el, whi[k], wlo[k], NT)
-        return 0
-
-    lax.fori_loop(0, nb, panel, 0)
+        eh, el = split(ec[:, span(k)])
+        z[:, span(k)] = dot3(eh, el, whi[k], wlo[k], NT)
+
+    panel(0)
+
+    @pl.loop(1, nb)
+    def _(k):
+        @pl.when(k == 1)
+        def _():
+            hooks[3]()
+
+        panel(k)
+
     for kk in range(nb - 1, -1, -1):
         cols = slice(kk * B, kk * B + B)
         zh, zl = split(z[:, cols])
@@ -218,35 +232,6 @@
         if kk > 0:
             xh, xl = split(x)
             z[:, : kk * B] -= dot3(xh, xl, lhi[cols, : kk * B], llo[cols, : kk * B], NN)
-
-
-def solve(a, eps):
-    n = eps.shape[0]
-    e = jnp.zeros((16, n), jnp.float32).at[0].set(eps)
-    nb = n // B
-    vm = pl.BlockSpec(memory_space=pltpu.VMEM)
-    return pl.pallas_call(
-        functools.partial(kernel, n),
-        out_shape=jax.ShapeDtypeStruct((16, n), jnp.float32),
-        in_specs=[pl.BlockSpec(memory_space=pl.ANY), vm],
-        out_specs=vm,
-        scratch_shapes=[
-            pltpu.VMEM((3, 6, n // 2 + B, H), jnp.float32),
-            pltpu.VMEM((n, n), jnp.bfloat16),
-            pltpu.VMEM((n, n), jnp.bfloat16),
-            pltpu.VMEM((16, n), jnp.float32),
-            pltpu.VMEM((nb, B, B), jnp.bfloat16),
-            pltpu.VMEM((nb, B, B), jnp.bfloat16),
-            pltpu.VMEM((H, H), jnp.float32),
-            pltpu.VMEM((2, H, H), jnp.float32),
-            pltpu.VMEM((128, H), jnp.float32),
-            pltpu.VMEM((16, H), jnp.float32),
-            pltpu.VMEM((128, H), jnp.float32),
-            pltpu.VMEM((16, n), jnp.float32),
-            pltpu.SemaphoreType.DMA,
-        ],
-        compiler_params=pltpu.CompilerParams(vmem_limit_bytes=56 * 2**20),
-    )(a, e)
 
 
 MESH = pl.DeviceIdType.MESH
@@ -298,9 +283,10 @@
     return pl.multiple_of(x, 8)
 
 
-def gram_kernel(total, x_ref, en_ref, O, xa, ebuf, F, recv, raw, xp, relay,
-                share_sem, c_send, c_recv, e_send, e_recv,
-                a_send, a_recv, own_sem):
+def kernel(total, x_ref, spin_ref, hop_ref, bond_ref, u_ref, c_ref, G, F, recv, raw, xa, xp, relay, spin, en_ref, ebuf,
+           lhi, llo, ec, whi, wlo, D, W, T, R, A2, z, x,
+           share_sem, c_send, c_recv, e_send, e_recv,
+           a_send, a_recv, own_sem, u_send, u_recv):
     pos, core = place()
     smp, par = lax.axis_index("smp"), lax.axis_index("par")
     n, kp = raw.shape
@@ -370,6 +356,16 @@
 
     scale = 1.0 / np.sqrt(np.float32(total))
 
+    def energy():
+        sites = spin_ref.shape[0]
+        spin[...] = jnp.zeros_like(spin)
+        spin[0:sites, :] = (2 * spin_ref[...] - 1).astype(jnp.float32)
+        sigma = spin[...]
+        field = lax.dot_general(bond_ref[...], sigma.astype(jnp.bfloat16), (NN, ((), ())), preferred_element_type=jnp.float32)
+        row = jnp.sum(sigma * field, axis=0, keepdims=True) + hop_ref[...]
+        en_ref[...] = jnp.broadcast_to(row, en_ref.shape)
+        ebuf[pl.ds(smp, 1)] = en_ref[...][None]
+
     def center(c):
         cols = slice(c * kc, (c + 1) * kc)
 
@@ -404,7 +400,7 @@
             at = (lax.div(j, 3), 2 * lax.rem(j, 3), pl.multiple_of(a_local * B, B))
             put(F, at, got if first else get(F, at) + got)
 
-    ebuf[pl.ds(smp, 1)] = en_ref[...][None]
+    energy()
     pl.semaphore_wait(barrier, len(peers))
     shares, moved = [], []
     spread = [remote(en_ref, ebuf.at[smp], e_send.at[d], e_recv.at[d], others[d]) for d in range(7)]
@@ -494,140 +490,148 @@
             copy.wait_recv()
             accumulate(q, base[q][4], size[4], offs[3] + d * size[4])
         at = pl.ds(eight(core * half + base[q][4]), size[4])
-        O[:, q, at, :] = F[:, q, pl.ds(eight(base[q][4]), size[4]), :]
-    def region(q, row, rows):
-        return part(O, q, core * half + row, rows)
-
-    def spread_out(q, stage):
-        here = region(q, base[q][stage + 3], size[stage + 3])
+        G[:, q, at, :] = F[:, q, pl.ds(eight(base[q][4]), size[4]), :]
+
+    early, late = slice(0, 1), slice(1, 3)
+
+    def region(q, some, row, rows):
+        return G.at[some, q, pl.ds(eight(core * half + row), rows), :]
+
+    def spread_out(q, some, stage):
+        here = region(q, some, base[q][stage + 3], size[stage + 3])
         return [go(here, here, who) for who in plans[q][1][stage][1]]
 
-    def double(q, t):
-        here = region(q, base[q][t + 1], size[t + 1])
+    def double(q, some, t):
+        here = region(q, some, base[q][t + 1], size[t + 1])
         return go(here, here, plans[q][0][t][0])
 
-    def across(q, row):
-        here = region(q, row, size[1])
+    def across(some):
+        here = G.at[some, :, pl.ds(pl.multiple_of(core * half, half), half), :]
         return go(here, here, partner)
 
-    five, six, seven, eighth, over = [], [], [], [], []
+    def arrive(copies):
+        for copy in copies:
+            copy.wait_recv()
+
+    def stage(name, some):
+        return {
+            "five": lambda q: spread_out(q, some, 1),
+            "six": lambda q: spread_out(q, some, 0),
+            "seven": lambda q: [double(q, some, 1)],
+            "eight": lambda q: [double(q, some, 0)],
+        }[name]
+
+    def follow(before, name, some):
+        out = []
+        for q in portions:
+            if before is not None:
+                arrive(before[q])
+            out.append(stage(name, some)(q))
+        return out
+
+    e5 = follow(None, "five", early)
+    l5 = follow(None, "five", late)
+    e6 = follow(e5, "six", early)
+    e7 = follow(e6, "seven", early)
+    l6 = follow(l5, "six", late)
+    e8 = follow(e7, "eight", early)
+    l7 = follow(l6, "seven", late)
     for q in portions:
-        five.append(spread_out(q, 1))
-    for q in portions:
-        for copy in five[q]:
-            copy.wait_recv()
-        six.append(spread_out(q, 0))
-    for q in portions:
-        for copy in six[q]:
-            copy.wait_recv()
-        seven.append(double(q, 1))
-    for q in portions:
-        seven[q].wait_recv()
-        eighth.append(double(q, 0))
-        over.append(across(q, base[q][1]))
-    for q in portions:
-        eighth[q].wait_recv()
-        over.append(across(q, size[1] - base[q][1]))
-    for copy in over:
-        copy.wait_recv()
-    for copy in pending:
-        copy.wait_send()
+        arrive(e8[q])
+    e9 = across(early)
+
     for copy in spread:
         copy.wait()
-    for copy in shares + moved:
-        copy.wait_send()
-
-
-def damped_gram(log_derivs, energy, total):
-    n, kp = total, log_derivs.shape[1] // 8
+    every = [ebuf[s, 0:1, :] for s in range(8)]
+    mean = sum(jnp.sum(row, axis=1, keepdims=True) for row in every) / total
+    ec[...] = jnp.zeros_like(ec)
+    for s in range(8):
+        ec[0:1, s * nr : (s + 1) * nr] = (every[s] - mean) * scale
+    e9.wait_recv()
+    flying = {}
+
+    def hook_one():
+        flying["l8"] = follow(l7, "eight", late)
+
+    def hook_two():
+        for q in portions:
+            arrive(flying["l8"][q])
+        flying["l9"] = across(late)
+
+    def hook_three():
+        flying["l9"].wait_recv()
+        for copy in pending + shares + moved:
+            copy.wait_send()
+
+    solve(n, x, G, lhi, llo, ec, whi, wlo, D, W, T, R, A2, z, [lambda: None, hook_one, hook_two, hook_three])
+
+    hi, lo = split(x[...])
+    d = lambda a: lax.dot_general(a, xa[...], (NN, ((), ())), preferred_element_type=jnp.float32)
+    u_ref[pl.ds(smp, 1)] = (d(hi) + d(lo))[0:8][None]
+    here = u_ref.at[smp]
+    final = [remote(here, here, u_send.at[i], u_recv.at[i], others[i]) for i in range(7)]
+    for copy in final:
+        copy.start()
+    c_ref[...] = x[0:8, pl.ds(pl.multiple_of(smp * nr, nr), nr)]
+    for copy in final:
+        copy.wait()
+
+
+SIDE = 10
+
+
+def bonds(size):
+    out = np.zeros((size, size), np.float32)
+    for r in range(SIDE):
+        for c in range(SIDE):
+            for dr, dc, weight in ((0, 1, 0.25), (1, 0, 0.25), (1, 1, 0.125), (1, -1, 0.125)):
+                out[r * SIDE + c, (r + dr) % SIDE * SIDE + (c + dc) % SIDE] += weight
+    return out
+
+
+def body(log_derivs, spins, hop_energy):
     nr = log_derivs.shape[0]
+    n, kp = nr * 8, log_derivs.shape[1] // 8
+    nb = n // B
     vm = pl.BlockSpec(memory_space=pltpu.VMEM)
     dma = pltpu.SemaphoreType.DMA
-    return pl.pallas_call(
-        functools.partial(gram_kernel, total),
-        out_shape=[
-            jax.ShapeDtypeStruct((3, PORTIONS, n // 2, H), jnp.float32),
-            jax.ShapeDtypeStruct((n, kp), jnp.bfloat16),
-            jax.ShapeDtypeStruct((8, 8, 128), jnp.float32),
-        ],
-        in_specs=[pl.BlockSpec(memory_space=pl.ANY), vm],
-        out_specs=[vm, vm, vm],
+    f32, bf16 = jnp.float32, jnp.bfloat16
+    u, coeffs = pl.pallas_call(
+        functools.partial(kernel, n),
+        out_shape=[jax.ShapeDtypeStruct((8, 8, kp), f32), jax.ShapeDtypeStruct((8, nr), f32)],
+        in_specs=[pl.BlockSpec(memory_space=pl.ANY), vm, vm, vm],
+        out_specs=[vm, vm],
         scratch_shapes=[
-            pltpu.VMEM((3, PORTIONS, n // 4, H), jnp.float32),
-            pltpu.VMEM((3, PORTIONS, n // 4, H), jnp.float32),
-            pltpu.VMEM((n, kp), jnp.bfloat16),
-            pltpu.VMEM((n, kp), jnp.bfloat16),
-            pltpu.VMEM((CHUNKS, 2, 2, nr // 2, kp // CHUNKS), jnp.bfloat16),
-            dma((CHUNKS, 2)), dma((18 * PORTIONS,)), dma((18 * PORTIONS,)), dma((7,)), dma((7,)),
-            dma((CHUNKS, 13)), dma((CHUNKS, 13)), dma((CHUNKS,)),
+            pltpu.VMEM((3, PORTIONS, n // 2 + B, H), f32),
+            pltpu.VMEM((3, PORTIONS, n // 4, H), f32),
+            pltpu.VMEM((3, PORTIONS, n // 4, H), f32),
+            pltpu.VMEM((n, kp), bf16),
+            pltpu.VMEM((n, kp), bf16),
+            pltpu.VMEM((n, kp), bf16),
+            pltpu.VMEM((CHUNKS, 2, 2, nr // 2, kp // CHUNKS), bf16),
+            pltpu.VMEM((H, nr), f32),
+            pltpu.VMEM((8, nr), f32),
+            pltpu.VMEM((8, 8, nr), f32),
+            pltpu.VMEM((n, n), bf16),
+            pltpu.VMEM((n, n), bf16),
+            pltpu.VMEM((16, n), f32),
+            pltpu.VMEM((nb, B, B), bf16),
+            pltpu.VMEM((nb, B, B), bf16),
+            pltpu.VMEM((H, H), f32),
+            pltpu.VMEM((2, H, H), f32),
+            pltpu.VMEM((128, H), f32),
+            pltpu.VMEM((16, H), f32),
+            pltpu.VMEM((128, H), f32),
+            pltpu.VMEM((16, n), f32),
+            pltpu.VMEM((16, n), f32),
+            dma((CHUNKS, 2)), dma((150,)), dma((150,)), dma((7,)), dma((7,)),
+            dma((CHUNKS, 13)), dma((CHUNKS, 13)), dma((CHUNKS,)), dma((7,)), dma((7,)),
         ],
         compiler_params=pltpu.CompilerParams(
-            vmem_limit_bytes=48 * 2**20, collective_id=1, has_side_effects=True
+            vmem_limit_bytes=58 * 2**20, collective_id=1, has_side_effects=True
         ),
-    )(log_derivs, energy)
-
-
-def update_kernel(x_ref, xc_ref, u_ref, send, recv):
-    smp, par = lax.axis_index("smp"), lax.axis_index("par")
-    others = [(lax.rem(smp + d, 8), par) for d in range(1, 8)]
-    barrier = pltpu.get_barrier_semaphore()
-    for who in others:
-        pl.semaphore_signal(barrier, inc=1, device_id=who, device_id_type=MESH)
-    hi, lo = split(x_ref[...])
-    d = lambda a: lax.dot_general(a, xc_ref[...], (NN, ((), ())), preferred_element_type=jnp.float32)
-    term = (d(hi) + d(lo))[0:8]
-    u_ref[pl.ds(smp, 1)] = term[None]
-    pl.semaphore_wait(barrier, len(others))
-    here = u_ref.at[smp]
-    copies = [remote(here, here, send.at[i], recv.at[i], others[i]) for i in range(7)]
-    for copy in copies:
-        copy.start()
-    for copy in copies:
-        copy.wait()
-
-
-def project(x, xc):
-    vm = pl.BlockSpec(memory_space=pltpu.VMEM)
-    u = pl.pallas_call(
-        update_kernel,
-        out_shape=jax.ShapeDtypeStruct((8, 8, xc.shape[1]), jnp.float32),
-        in_specs=[vm, vm],
-        out_specs=vm,
-        scratch_shapes=[pltpu.SemaphoreType.DMA((7,)), pltpu.SemaphoreType.DMA((7,))],
-        compiler_params=pltpu.CompilerParams(
-            vmem_limit_bytes=32 * 2**20, collective_id=2, has_side_effects=True
-        ),
-    )(x, xc)
-    return u[:, 0, :].reshape(-1)
-
-
-SIDE = 10
-
-
-def local_energy(spins):
-    sigma = (2 * spins - 1).astype(jnp.float32).reshape(-1, SIDE, SIDE)
-    right = jnp.roll(sigma, 1, axis=2)
-    below = jnp.roll(sigma, 1, axis=1)
-    diag_one = jnp.roll(below, 1, axis=2)
-    diag_two = jnp.roll(below, -1, axis=2)
-    nearest = jnp.sum(sigma * right + sigma * below, axis=(1, 2))
-    second = jnp.sum(sigma * diag_one + sigma * diag_two, axis=(1, 2))
-    return 0.25 * nearest + 0.125 * second
-
-
-def body(log_derivs, spins, hop_energy):
-    rows = log_derivs.shape[0]
-    total = rows * 8
-    scale = 1.0 / jnp.sqrt(jnp.float32(total))
-    energy = local_energy(spins) + hop_energy
-    energy = jnp.pad(energy.reshape(rows // 128, 128), ((0, 8 - rows // 128), (0, 0)))
-    gram, centered, energies = damped_gram(log_derivs, energy, total)
-    all_energy = energies[:, : rows // 128].reshape(-1)
-    eps = (all_energy - jnp.mean(all_energy)) * scale
-    coeffs = solve(gram, eps)
-    update = project(coeffs, centered)
-    start = lax.axis_index("smp") * rows
-    return update, lax.dynamic_slice_in_dim(coeffs[0], start, rows, 0)
+    )(log_derivs, spins.T, hop_energy[None], jnp.asarray(bonds(H), bf16))
+    return u[:, 0, :].reshape(-1), coeffs[0]
 
 
 def solution(mesh):

time: 201 us -> 190 us (0.945)
  Pallas kernels: 193 us -> 187 us
    pallas_call x3 -> x1, Pallas kernels: 193 us -> 187 us  [body(): pl.pallas_call(functools.partial(kernel, n), out_shape=[jax.ShapeDtypeStr...]
    unnamed x8 -> x0, local copies, waits for them, and re-layouts: 2.49 us -> none
    slice x6 -> x2, local copies, waits for them, and re-layouts: 0.64 us -> 2.78 us  [body(): return (u[:, 0, :].reshape(-1), coeffs[0])]
where the time goes in v6:
time: 190 us
  Pallas kernels  187 us (98%)
  local copies, waits for them, and re-layouts  2.78 us (1%)
    pallas_call x1, Pallas kernels, body(): pl.pallas_call(functools.partial(kernel, n), out_shape=[jax.ShapeDtypeStr...  187 us

profile of v6, /device:TPU:1, one launch (start us, length us, event | category | flops | bytes accessed | tf_op | source)
XLA Modules:
  0.0 190.2 jit_solution(206759608470053167)
XLA Ops:
  0.6 186.7 %shard_map.59 = (f32[8,8,512]{2,1,0:T(8,128)}, f32[8,256]{1,0:T(8,128)}) custom-call(bf16[256,4096]{1,0:T(8,128)(2,1)} %x_ref.1, s32[100,256]{1,0:T(8,128)} %bitcast.4, f32[1,256]{1,0:T(1,128)} %bitcast.6, bf16[128,128]{1,0:T(8,128)(2,1)} %constant.2.clone.bond_ref), custom_call_target="tpu_custom_call" | custom-call | tf_op jit(solution)/shard_map/pallas_call | solution.py:599
  187.4 1.5 slice.6
  188.9 1.3 slice.7

commit v7 on v6

--- a/solution.py
+++ b/solution.py
@@ -20,6 +20,13 @@
 def dot3(ah, al, bh, bl, dims):
     d = lambda a, b: lax.dot_general(a, b, (dims, ((), ())), preferred_element_type=jnp.float32)
     return d(ah, bh) + (d(ah, bl) + d(al, bh))
+
+
+def thin(x, bh, bl, dims):
+    xh, xl = split(x)
+    d = lambda a, b: lax.dot_general(a, b, (dims, ((), ())), preferred_element_type=jnp.float32)
+    both = d(jnp.concatenate([xh, xl], axis=0), bh)
+    return both[0:16] + (both[16:32] + d(xh, bl))
 
 
 def splat(x):
@@ -93,14 +100,38 @@
     return [jnp.where(lane <= sub + 8 * g, out[g], 0.0) for g in range(16)]
 
 
+def known(*xs):
+    return all(isinstance(x, int) for x in xs)
+
+
+def div(a, b):
+    return a // b if known(a, b) else lax.div(jnp.int32(a), jnp.int32(b))
+
+
+def rem(a, b):
+    return a % b if known(a, b) else lax.rem(jnp.int32(a), jnp.int32(b))
+
+
+def least(a, b):
+    return min(a, b) if known(a, b) else jnp.minimum(a, b)
+
+
+def choose(c, a, b):
+    return (a if c else b) if isinstance(c, bool) else jnp.where(c, a, b)
+
+
+def multiple(x, m):
+    return x if known(x) else pl.multiple_of(x, m)
+
+
 def slot(nb, i, k):
-    return nb * k - lax.div(k * (k - 1), 2) + i - k
+    return nb * k - div(k * (k - 1), 2) + i - k
 
 
 def tile(nb, i, k):
     t = slot(nb, i, k)
-    a, j = lax.rem(t, PACK), lax.div(t, PACK)
-    return lax.div(j, 3), 2 * lax.rem(j, 3), pl.multiple_of(a * B, B)
+    a, j = rem(t, PACK), div(t, PACK)
+    return div(j, 3), 2 * rem(j, 3), multiple(a * B, B)
 
 
 def get(G, at):
@@ -121,10 +152,10 @@
 
 
 def block(i):
-    return pl.ds(pl.multiple_of(i * B, B), B)
-
-
-SLOTS = 8
+    return pl.ds(multiple(i * B, B), B)
+
+
+TRIANGLES = 6
 PACK = 4
 
 
@@ -136,27 +167,29 @@
     def span(k):
         return slice(k * B, k * B + B) if isinstance(k, int) else block(k)
 
-    def triangle(k, i):
+    def triangle(k, i, live):
         ch, cl = split(get(G, tile(nb, i, k)))
         th, tl = split(dot3(ch, cl, whi[k], wlo[k], NT))
         lhi[block(i), span(k)], llo[block(i), span(k)] = th, tl
-        yh, yl = split(z[:, span(k)])
-        ec[:, block(i)] -= dot3(yh, yl, th, tl, NT)
+        ec[:, block(i)] -= thin(z[:, span(k)], th, tl, NT) * live
         return th, tl
 
     def factor(k, h, slots):
         def beside(p):
-            if p % (16 // SLOTS) != 0:
+            if h == 0 and p < TRIANGLES:
+                triangle(k - 1, least(k + 1 + p, nb - 1), choose(k + 1 + p < nb, 1.0, 0.0))
                 return
-            s = h * SLOTS + p // (16 // SLOTS)
+            if h == 0 and (p - TRIANGLES) % 2 != 0 or h == 1 and p >= 11:
+                return
+            s = (p - TRIANGLES) // 2 if h == 0 else 5 + p
             live = s < (k + 1) * (nb - 1 - k)
-            i = jnp.minimum(k + 1 + lax.div(s, k + 1), nb - 1)
-            u = lax.rem(s, k + 1)
+            i = least(k + 1 + div(s, k + 1), nb - 1)
+            u = rem(s, k + 1)
             own = u == k
-            column = jnp.where(own, k, jnp.minimum(k + 1, nb - 1))
-            j = jnp.where(own, k - 1, u)
+            column = choose(own, k, least(k + 1, nb - 1))
+            j = choose(own, k - 1, u)
             at = tile(nb, i, column)
-            at = (at[0], at[1], pl.multiple_of(jnp.where(live, at[2], n // 2), B))
+            at = (at[0], at[1], multiple(choose(live, at[2], n // 2), B))
             sub(G, at, dot3(
                 lhi[block(i), block(j)], llo[block(i), block(j)],
                 lhi[block(column), block(j)], llo[block(column), block(j)], NT))
@@ -167,7 +200,7 @@
 
     def chain(k, h):
         if isinstance(k, int):
-            factor(k, h, False)
+            factor(k, h, k > 0)
             return
 
         @pl.when(k < nb - 1)
@@ -178,25 +211,22 @@
         def _():
             factor(k, h, False)
 
+    def at_place(k, place):
+        if known(k) and (k, place) in hooks:
+            hooks[k, place]()
+
     def panel(k):
-        first = isinstance(k, int)
-        home = (0, 0, 0) if first else tile(nb, k, k)
-        if not first:
-            th, tl = triangle(k - 1, k)
+        home = tile(nb, k, k)
+        if not (known(k) and k == 0):
+            th, tl = triangle(k - 1, k, 1.0)
             sub(G, home, dot3(th, tl, th, tl, NT))
 
-            @pl.loop(k + 1, nb)
-            def _(i):
-                triangle(k - 1, i)
-
+        at_place(k, 0)
         hs, hq, hr = home
-        top, low = (pl.ds(0, H), pl.ds(H, H)) if first else (pl.ds(hr, H), pl.ds(pl.multiple_of(hr + H, H), H))
+        top, low = pl.ds(hr, H), pl.ds(multiple(hr + H, H), H)
         D[...] = G[hs, hq, top, :] + damp
-        if first:
-            hooks[0]()
         chain(k, 0)
-        if first:
-            hooks[1]()
+        at_place(k, 1)
         w1h, w1l = split(W[0])
         ah, al = split(G[hs, hq, low, :])
         lh, ll = split(dot3(ah, al, w1h, w1l, NT))
@@ -206,32 +236,25 @@
         whi[k, 0:H, H:B] = jnp.zeros((H, H), jnp.bfloat16)
         wlo[k, 0:H, H:B] = jnp.zeros((H, H), jnp.bfloat16)
         chain(k, 1)
-        if first:
-            hooks[2]()
         w2h, w2l = split(W[1])
         whi[k, H:B, H:B], wlo[k, H:B, H:B] = w2h, w2l
         whi[k, H:B, 0:H], wlo[k, H:B, 0:H] = split(-dot3(w2h, w2l, th, tl, NN))
-        eh, el = split(ec[:, span(k)])
-        z[:, span(k)] = dot3(eh, el, whi[k], wlo[k], NT)
+        z[:, span(k)] = thin(ec[:, span(k)], whi[k], wlo[k], NT)
+        at_place(k, 2)
 
     panel(0)
-
-    @pl.loop(1, nb)
+    panel(1)
+
+    @pl.loop(2, nb)
     def _(k):
-        @pl.when(k == 1)
-        def _():
-            hooks[3]()
-
         panel(k)
 
     for kk in range(nb - 1, -1, -1):
         cols = slice(kk * B, kk * B + B)
-        zh, zl = split(z[:, cols])
-        x = dot3(zh, zl, whi[kk], wlo[kk], NN)
+        x = thin(z[:, cols], whi[kk], wlo[kk], NN)
         x_ref[:, cols] = x
         if kk > 0:
-            xh, xl = split(x)
-            z[:, : kk * B] -= dot3(xh, xl, lhi[cols, : kk * B], llo[cols, : kk * B], NN)
+            z[:, : kk * B] -= thin(x, lhi[cols, : kk * B], llo[cols, : kk * B], NN)
 
 
 MESH = pl.DeviceIdType.MESH
@@ -283,7 +306,7 @@
     return pl.multiple_of(x, 8)
 
 
-def kernel(total, x_ref, spin_ref, hop_ref, bond_ref, u_ref, c_ref, G, F, recv, raw, xa, xp, relay, spin, en_ref, ebuf,
+def kernel(total, x_ref, spin_ref, hop_ref, bond_ref, o_ref, c_ref, u_ref, G, F, recv, raw, xa, xp, relay, spin, en_ref, ebuf,
            lhi, llo, ec, whi, wlo, D, W, T, R, A2, z, x,
            share_sem, c_send, c_recv, e_send, e_recv,
            a_send, a_recv, own_sem, u_send, u_recv):
@@ -492,7 +515,7 @@
         at = pl.ds(eight(core * half + base[q][4]), size[4])
         G[:, q, at, :] = F[:, q, pl.ds(eight(base[q][4]), size[4]), :]
 
-    early, late = slice(0, 1), slice(1, 3)
+    early, late = slice(0, 2), slice(2, 3)
 
     def region(q, some, row, rows):
         return G.at[some, q, pl.ds(eight(core * half + row), rows), :]
@@ -530,15 +553,15 @@
         return out
 
     e5 = follow(None, "five", early)
-    l5 = follow(None, "five", late)
     e6 = follow(e5, "six", early)
     e7 = follow(e6, "seven", early)
-    l6 = follow(l5, "six", late)
     e8 = follow(e7, "eight", early)
-    l7 = follow(l6, "seven", late)
+    own = len(pending)
+    l5 = follow(None, "five", late)
     for q in portions:
         arrive(e8[q])
-    e9 = across(early)
+    e9, f9 = across(slice(0, 1)), across(slice(1, 2))
+    early_sends = pending[:own] + pending[-2:]
 
     for copy in spread:
         copy.wait()
@@ -550,20 +573,31 @@
     e9.wait_recv()
     flying = {}
 
-    def hook_one():
-        flying["l8"] = follow(l7, "eight", late)
-
-    def hook_two():
+    def six():
+        flying[6] = follow(l5, "six", late)
+
+    def seven():
+        flying[7] = follow(flying[6], "seven", late)
+
+    def eight_():
+        flying[8] = follow(flying[7], "eight", late)
+        f9.wait_recv()
+        for copy in early_sends + shares + moved:
+            copy.wait_send()
+
+    def nine():
         for q in portions:
-            arrive(flying["l8"][q])
-        flying["l9"] = across(late)
-
-    def hook_three():
-        flying["l9"].wait_recv()
-        for copy in pending + shares + moved:
-            copy.wait_send()
-
-    solve(n, x, G, lhi, llo, ec, whi, wlo, D, W, T, R, A2, z, [lambda: None, hook_one, hook_two, hook_three])
+            arrive(flying[8][q])
+        flying[9] = across(late)
+
+    def rest():
+        flying[9].wait_recv()
+        for copy in pending:
+            if all(copy is not other for other in early_sends):
+                copy.wait_send()
+
+    hooks = {(0, 0): six, (0, 1): seven, (0, 2): eight_, (1, 1): nine, (1, 2): rest}
+    solve(n, x, G, lhi, llo, ec, whi, wlo, D, W, T, R, A2, z, hooks)
 
     hi, lo = split(x[...])
     d = lambda a: lax.dot_general(a, xa[...], (NN, ((), ())), preferred_element_type=jnp.float32)
@@ -572,9 +606,11 @@
     final = [remote(here, here, u_send.at[i], u_recv.at[i], others[i]) for i in range(7)]
     for copy in final:
         copy.start()
-    c_ref[...] = x[0:8, pl.ds(pl.multiple_of(smp * nr, nr), nr)]
+    c_ref[...] = x[0:1, pl.ds(pl.multiple_of(smp * nr, nr), nr)]
     for copy in final:
         copy.wait()
+    for s in range(8):
+        o_ref[0:1, s * kp : (s + 1) * kp] = u_ref[s, 0:1, :]
 
 
 SIDE = 10
@@ -598,10 +634,11 @@
     f32, bf16 = jnp.float32, jnp.bfloat16
     u, coeffs = pl.pallas_call(
         functools.partial(kernel, n),
-        out_shape=[jax.ShapeDtypeStruct((8, 8, kp), f32), jax.ShapeDtypeStruct((8, nr), f32)],
+        out_shape=[jax.ShapeDtypeStruct((1, 8 * kp), f32), jax.ShapeDtypeStruct((1, nr), f32)],
         in_specs=[pl.BlockSpec(memory_space=pl.ANY), vm, vm, vm],
         out_specs=[vm, vm],
         scratch_shapes=[
+            pltpu.VMEM((8, 8, kp), f32),
             pltpu.VMEM((3, PORTIONS, n // 2 + B, H), f32),
             pltpu.VMEM((3, PORTIONS, n // 4, H), f32),
             pltpu.VMEM((3, PORTIONS, n // 4, H), f32),
@@ -631,7 +668,7 @@
             vmem_limit_bytes=58 * 2**20, collective_id=1, has_side_effects=True
         ),
     )(log_derivs, spins.T, hop_energy[None], jnp.asarray(bonds(H), bf16))
-    return u[:, 0, :].reshape(-1), coeffs[0]
+    return u.reshape(-1), coeffs.reshape(-1)
 
 
 def solution(mesh):

time: 190 us -> 177 us (0.932)
  Pallas kernels: 187 us -> 174 us
    pallas_call x1, Pallas kernels: 187 us -> 174 us  [body(): pl.pallas_call(functools.partial(kernel, n), out_shape=[jax.ShapeDtypeStr...]
    slice x2 -> x0, local copies, waits for them, and re-layouts: 2.78 us -> none  [body(): return (u[:, 0, :].reshape(-1), coeffs[0])]
    unnamed x0 -> x2, local copies, waits for them, and re-layouts: none -> 2.54 us
where the time goes in v7:
time: 177 us
  Pallas kernels  174 us (98%)
  local copies, waits for them, and re-layouts  2.54 us (1%)
    pallas_call x1, Pallas kernels, body(): pl.pallas_call(functools.partial(kernel, n), out_shape=[jax.ShapeDtypeStr...  174 us

profile of v7, /device:TPU:1, one launch (start us, length us, event | category | flops | bytes accessed | tf_op | source)
XLA Modules:
  0.0 176.9 jit_solution(1497776615049403911)
XLA Ops:
  0.6 173.7 %shard_map.59 = (f32[1,4096]{1,0:T(1,128)}, f32[1,256]{1,0:T(1,128)}) custom-call(bf16[256,4096]{1,0:T(8,128)(2,1)} %x_ref.1, s32[100,256]{1,0:T(8,128)} %bitcast.4, f32[1,256]{1,0:T(1,128)} %bitcast.6, bf16[128,128]{1,0:T(8,128)(2,1)} %constant.2.clone.bond_ref), custom_call_target="tpu_custom_call" | custom-call | tf_op jit(solution)/shard_map/pallas_call | solution.py:635
  174.4 1.3 copy.8
  175.7 1.2 copy.9

commit v8 on v7

--- a/solution.py
+++ b/solution.py
@@ -427,12 +427,11 @@
     pl.semaphore_wait(barrier, len(peers))
     shares, moved = [], []
     spread = [remote(en_ref, ebuf.at[smp], e_send.at[d], e_recv.at[d], others[d]) for d in range(7)]
-    flight = begin(0)
+    legs, direct, own = begin(0)
+    onward = pass_on(0, legs)
     for c in range(CHUNKS):
-        legs, direct, own = flight
-        onward = pass_on(c, legs)
         if c + 1 < CHUNKS:
-            flight = begin(c + 1)
+            later = begin(c + 1)
         else:
             for copy in spread:
                 copy.start()
@@ -441,6 +440,9 @@
         own.wait()
         moved += legs + direct + onward
         shares.append(center(c))
+        if c + 1 < CHUNKS:
+            legs, direct, own = later
+            onward = pass_on(c + 1, legs)
         tiles(xa, c, c == 0)
         shares[c].wait_recv()
         tiles(xp, c, False)

time: 177 us -> 174 us (0.983)
  Pallas kernels: 174 us -> 170 us
    pallas_call x1, Pallas kernels: 174 us -> 170 us  [body(): pl.pallas_call(functools.partial(kernel, n), out_shape=[jax.ShapeDtypeStr...]
where the time goes in v8:
time: 174 us; the launch traced here: 173 us
  Pallas kernels  170 us (98%)
  local copies, waits for them, and re-layouts  2.54 us (1%)
    pallas_call x1, Pallas kernels, body(): pl.pallas_call(functools.partial(kernel, n), out_shape=[jax.ShapeDtypeStr...  170 us

profile of v8, /device:TPU:1, one launch (start us, length us, event | category | flops | bytes accessed | tf_op | source)
XLA Modules:
  0.0 173.5 jit_solution(15549213358653390319)
XLA Ops:
  0.6 170.3 %shard_map.59 = (f32[1,4096]{1,0:T(1,128)}, f32[1,256]{1,0:T(1,128)}) custom-call(bf16[256,4096]{1,0:T(8,128)(2,1)} %x_ref.1, s32[100,256]{1,0:T(8,128)} %bitcast.4, f32[1,256]{1,0:T(1,128)} %bitcast.6, bf16[128,128]{1,0:T(8,128)(2,1)} %constant.2.clone.bond_ref), custom_call_target="tpu_custom_call" | custom-call | tf_op jit(solution)/shard_map/pallas_call | solution.py:637
  170.9 1.3 copy.8
  172.3 1.2 copy.9
